TPU v7x, 256 devices: a whole 4x4x8 slice. The times are simulated.
256 devices in a mesh: row: 16 (over z_hi, y), col: 16 (over x, z_lo, core).
Axes of the slice: x: 4, y: 4, z: 8 (z_hi: 4, z_lo: 2; z = z_hi * 2 + z_lo), core: 2. Of those that a mesh axis runs over, the one named last changes fastest.
Arguments:
- elevation: float32 [8192, 16384], P('row', 'col'), may hold values from -20 to 20
- start_controls: float32 [2048, 4096], P('row', 'col'), may hold values from -6 to 6
Outputs:
- controls: float32 [2048, 4096], P('row', 'col')
- residual: float32 [2048, 4096], P('row', 'col')
All inputs are finite; a program needn't handle non-finite values.
Results may differ from a plain program's by a relative error of at most 0.0003.
Values sent between devices are 32-bit elements; how exact they have to be, the bound alone decides.
A program may use at most 64 MiB of HBM per device.

v0:
```python
import jax
import jax.numpy as jnp
from jax import lax
from jax.sharding import PartitionSpec as P

ITERS = 3


huber_delta = 1.5
ridge = 0.25


def from_behind(block, axis, distance):
    devices = range(lax.axis_size(axis))
    route = [(i - distance, i) for i in devices if i - distance in devices]
    return lax.ppermute(block, axis, route)


def cubic(fraction):
    rest = 1.0 - fraction
    cube = fraction * fraction * fraction
    square = fraction * fraction
    return (
        rest * rest * rest / 6.0,
        (3.0 * cube - 6.0 * square + 4.0) / 6.0,
        (-3.0 * cube + 3.0 * square + 3.0 * fraction + 1.0) / 6.0,
        cube / 6.0,
    )


def spline_table():
    return [list(cubic((phase + 0.5) / 4.0)) for phase in range(4)]


def expand_rows(field, table):
    count = field.shape[0] - 3
    outputs = []
    for phase in range(4):
        total = table[phase][0] * field[0:count]
        for offset in range(1, 4):
            total = total + table[phase][offset] * field[offset : offset + count]
        outputs.append(total)
    return jnp.stack(outputs, axis=1).reshape(4 * count, field.shape[1])


def expand_cols(field, table):
    count = field.shape[1] - 3
    outputs = []
    for phase in range(4):
        total = table[phase][0] * field[:, 0:count]
        for offset in range(1, 4):
            total = total + table[phase][offset] * field[:, offset : offset + count]
        outputs.append(total)
    return jnp.stack(outputs, axis=2).reshape(field.shape[0], 4 * count)


def reduce_rows(field, table):
    count = field.shape[0] // 4
    grouped = field.reshape(count, 4, field.shape[1])
    total = None
    for offset in range(4):
        part = table[0][offset] * grouped[:, 0]
        for phase in range(1, 4):
            part = part + table[phase][offset] * grouped[:, phase]
        placed = jnp.pad(part, ((offset, 3 - offset), (0, 0)))
        total = placed if total is None else total + placed
    return total


def reduce_cols(field, table):
    count = field.shape[1] // 4
    grouped = field.reshape(field.shape[0], count, 4)
    total = None
    for offset in range(4):
        part = table[0][offset] * grouped[:, :, 0]
        for phase in range(1, 4):
            part = part + table[phase][offset] * grouped[:, :, phase]
        placed = jnp.pad(part, ((0, 0), (offset, 3 - offset)))
        total = placed if total is None else total + placed
    return total


def extend(tile):
    below = from_behind(tile[:3], "row", -1)
    taller = jnp.concatenate([tile, below], 0)
    beside = from_behind(taller[:, :3], "col", -1)
    return jnp.concatenate([taller, beside], 1)


def fold(partial_value):
    tile_rows = partial_value.shape[0] - 3
    tile_cols = partial_value.shape[1] - 3
    beside = from_behind(partial_value[:, tile_cols:], "col", 1)
    narrow = jnp.concatenate([partial_value[:, :3] + beside, partial_value[:, 3:tile_cols]], 1)
    below = from_behind(narrow[tile_rows:], "row", 1)
    return jnp.concatenate([narrow[:3] + below, narrow[3:tile_rows]], 0)


def squares(residual):
    return lax.psum(jnp.sum(residual * residual), ("row", "col"))


def shards(elevation, start_controls):
    table = spline_table()

    def evaluate(tile):
        return expand_cols(expand_rows(extend(tile), table), table)

    def transposed(field):
        return fold(reduce_rows(reduce_cols(field, table), table))

    misfit = elevation - evaluate(start_controls)
    weights = huber_delta / jnp.maximum(jnp.abs(misfit), huber_delta)
    first_term = transposed(weights * misfit)
    controls = start_controls
    residual = first_term - ridge * start_controls
    direction = residual
    norm_now = squares(residual)
    for step in range(ITERS):
        image = transposed(weights * evaluate(direction)) + ridge * direction
        alpha = norm_now / lax.psum(jnp.sum(direction * image), ("row", "col"))
        controls = controls + alpha * direction
        residual = residual - alpha * image
        norm_next = squares(residual)
        direction = residual + norm_next / norm_now * direction
        norm_now = norm_next
    return (controls, residual)


def solution(mesh):
    return jax.shard_map(
        shards,
        mesh=mesh,
        in_specs=(P("row", "col"), P("row", "col")),
        out_specs=(P("row", "col"), P("row", "col")),
        check_vma=False,
    )
```

profile of v0, /device:TPU:1, one launch (start us, length us, event | category | flops | bytes accessed | tf_op | source)
XLA Modules:
  0.0 665.8 jit_solution(7773680915069925878)
XLA Ops:
  3.8 4.1 collective-permute-done
  7.9 5.6 collective-permute-start.1
  20.4 3.1 copy.1751
  23.5 3.0 reshape.405
  26.4 3.5 subtract_multiply_fusion
  32.7 6.7 %fusion.28 = (f32[512,256,1]{0,2,1:T(1,128)S(1)}, f32[512,256,1]{0,2,1:T(1,128)}, f32[512,256,1]{0,2,1:T(1,128)}, f32[512,256,1]{0,2,1:T(1,128)}) fusion(f32[512,256,4]{0,2,1:T(4,128)} %reshape.406), kind=kLoop, calls=%fused_computation.181 | loop fusion | bytes 4194304 | tf_op jit(solution)/shard_map/slice | solution.py:75
  60.7 3.0 collective-permute-done.3
  65.0 6.0 collective-permute-done.4
  71.1 3.6 collective-permute-start.5
  81.2 3.1 copy.1763
  84.3 3.0 reshape.409
  87.3 4.3 fusion.22
  94.4 6.9 %fusion.27 = (f32[512,256,1]{0,2,1:T(1,128)}, f32[512,256,1]{0,2,1:T(1,128)}, f32[512,256,1]{0,2,1:T(1,128)}, f32[512,256,1]{0,2,1:T(1,128)}) fusion(f32[512,256,4]{0,2,1:T(4,128)} %reshape.410), kind=kLoop, calls=%fused_computation.180 | loop fusion | bytes 4194304 | tf_op jit(solution)/shard_map/slice | solution.py:75
  123.8 7.0 %collective-permute-start.7 = (f32[3,256]{0,1:T(8,128)S(1)}, f32[3,256]{0,1:T(8,128)S(1)}, u32[]{:S(2)}, u32[]{:S(2)}) collective-permute-start(f32[3,256]{0,1:T(8,128)S(1)} %fusion.6), channel_id=1, source_target_pairs={{0,16},{16,32},{32,48},{48,64},{64,80},{80,96},{96,112},{112,128},... | collective-permute-start | bytes 9224 | tf_op jit(solution)/shard_map/ppermute | solution.py:16
  134.2 91.6 %all-reduce.32 = (f32[]{:T(128)}, f32[]{:T(128)}) all-reduce(f32[]{:T(128)} %get-tuple-element.7, f32[]{:T(128)} %get-tuple-element.6), channel_id=1, replica_groups=mesh['row'=16,'col'=16] {'row','col'}, use_global_device_ids=true, to_apply=%region_1.2 | all-reduce | flops 2 | bytes 16 | tf_op jit(solution)/shard_map/psum | solution.py:100
  227.8 72.6 %psum.44 = f32[]{:T(128)} all-reduce(f32[]{:T(128)} %multiply_reduce_fusion.3), channel_id=1, replica_groups=mesh['row'=16,'col'=16] {'row','col'}, use_global_device_ids=true, to_apply=%region_5.6 | all-reduce | flops 1 | bytes 8 | tf_op jit(solution)/shard_map/psum | solution.py:100
  303.3 4.8 collective-permute-done.8
  308.1 3.4 collective-permute-start.9
  311.5 2.9 collective-permute-done.9
  319.5 3.1 copy.1774
  322.5 3.0 reshape.413
  325.5 4.3 fusion.21
  332.7 6.9 %fusion.26 = (f32[512,256,1]{0,2,1:T(1,128)}, f32[512,256,1]{0,2,1:T(1,128)}, f32[512,256,1]{0,2,1:T(1,128)}, f32[512,256,1]{0,2,1:T(1,128)}) fusion(f32[512,256,4]{0,2,1:T(4,128)} %reshape.414), kind=kLoop, calls=%fused_computation.179 | loop fusion | bytes 4194304 | tf_op jit(solution)/shard_map/slice | solution.py:75
  361.4 3.0 collective-permute-start.11
  367.8 84.8 %psum.45 = f32[]{:T(128)} all-reduce(f32[]{:T(128)} %multiply_reduce_fusion.2), channel_id=1, replica_groups=mesh['row'=16,'col'=16] {'row','col'}, use_global_device_ids=true, to_apply=%region_7.8 | all-reduce | flops 1 | bytes 8 | tf_op jit(solution)/shard_map/psum | solution.py:121
  454.6 72.6 %psum.46 = f32[]{:T(128)} all-reduce(f32[]{:T(128)} %get-tuple-element.12), channel_id=1, replica_groups=mesh['row'=16,'col'=16] {'row','col'}, use_global_device_ids=true, to_apply=%region_9.10 | all-reduce | flops 1 | bytes 8 | tf_op jit(solution)/shard_map/psum | solution.py:100
  530.1 5.0 collective-permute-done.12
  535.1 3.4 collective-permute-start.13
  546.5 3.1 copy.1784
  549.5 3.0 reshape.417
  552.5 4.3 fusion.20
  577.8 84.8 %psum.47 = f32[]{:T(128)} all-reduce(f32[]{:T(128)} %get-tuple-element.10), channel_id=1, replica_groups=mesh['row'=16,'col'=16] {'row','col'}, use_global_device_ids=true, to_apply=%region_11.12 | all-reduce | flops 1 | bytes 8 | tf_op jit(solution)/shard_map/psum | solution.py:121
  (163 shorter events, 138.2 us)
Async XLA Ops:
  1.5 6.4 collective-permute-start
  7.9 7.6 %collective-permute-start.1 = (f32[131,3]{0,1:T(4,128)S(1)}, f32[131,3]{0,1:T(4,128)S(1)}, u32[]{:S(2)}, u32[]{:S(2)}) collective-permute-start(f32[131,3]{0,1:T(4,128)S(1)} %pad_maximum_fusion.15), channel_id=1, source_target_pairs={{1,0},{2,1},{3,2},{4,3},{5,4},{6,5},{7,6},{8,7},{9,8},{10,9},{11,1... | collective-permute-start | bytes 4724 | tf_op jit(solution)/shard_map/ppermute | solution.py:16
  54.6 3.1 collective-permute-start.2
  57.8 5.9 collective-permute-start.3
  63.7 7.3 %collective-permute-start.4 = (f32[3,256]{0,1:T(8,128)S(1)}, f32[3,256]{0,1:T(8,128)S(1)}, u32[]{:S(2)}, u32[]{:S(2)}) collective-permute-start(f32[3,256]{0,1:T(8,128)S(1)} %bitcast.159), channel_id=1, source_target_pairs={{16,0},{32,16},{48,32},{64,48},{80,64},{96,80},{112,96},{128,112},... | collective-permute-start | bytes 9224 | tf_op jit(solution)/shard_map/ppermute | solution.py:16
  71.1 5.2 collective-permute-start.5
  120.6 3.1 collective-permute-start.6
  123.8 9.7 %collective-permute-start.7 = (f32[3,256]{0,1:T(8,128)S(1)}, f32[3,256]{0,1:T(8,128)S(1)}, u32[]{:S(2)}, u32[]{:S(2)}) collective-permute-start(f32[3,256]{0,1:T(8,128)S(1)} %fusion.6), channel_id=1, source_target_pairs={{0,16},{16,32},{32,48},{48,64},{64,80},{80,96},{96,112},{112,128},... | collective-permute-start | bytes 9224 | tf_op jit(solution)/shard_map/ppermute | solution.py:16
  301.8 6.3 collective-permute-start.8
  308.1 6.4 collective-permute-start.9
  358.3 3.1 collective-permute-start.10
  361.4 5.7 collective-permute-start.11
  528.6 6.5 collective-permute-start.12
  535.1 6.4 collective-permute-start.13
  561.5 2.6 copy-start.1
  561.5 3.1 copy-start
  569.0 3.1 collective-permute-start.14
  572.1 5.0 collective-permute-start.15
where the time goes:
time: 676 us; the launch traced here: 666 us
  blocking collectives  406 us (60%)
  local copies, waits for them, and re-layouts  117 us (17%)
  other arithmetic  47.9 us (7%)
  starting transfers between devices  44.5 us (7%)
  waiting for transfers between devices  41.8 us (6%)
  between operations  8.28 us (1%)
    psum x3, blocking collectives, squares(): return lax.psum(jnp.sum(residual * residual), ('row', 'col'))  237 us
    psum x2, blocking collectives, shards(): alpha = norm_now / lax.psum(jnp.sum(direction * image), ('row', 'col'))  170 us
    ppermute x16, starting transfers between devices, from_behind(): return lax.ppermute(block, axis, route)  44.5 us
    ppermute x16, waiting for transfers between devices, from_behind(): return lax.ppermute(block, axis, route)  41.8 us
    unnamed x54, local copies, waits for them, and re-layouts  39.1 us
    slice x4, local copies, waits for them, and re-layouts, reduce_cols(): part = table[0][offset] * grouped[:, :, 0]  23.2 us
  transfers between devices with their start and end apart: 16, of which 15 were waited for; matrix products, arithmetic and copies ran while one was open for 1% of the time, Pallas kernels for 0%

commit v1 on v0

v1 whole, which is shorter than its diff:
```python
import functools

import jax
import jax.numpy as jnp
from jax import lax
from jax.experimental import pallas as pl
from jax.experimental.pallas import tpu as pltpu
from jax.sharding import PartitionSpec as P

MESH = pl.DeviceIdType.MESH
F32 = jnp.float32
BF16 = jnp.bfloat16
huber_delta = 1.5
ridge = 0.25

PAD = 16
LANES = 128


def cubic(fraction):
    rest = 1.0 - fraction
    cube = fraction * fraction * fraction
    square = fraction * fraction
    return (
        rest * rest * rest / 6.0,
        (3.0 * cube - 6.0 * square + 4.0) / 6.0,
        (-3.0 * cube + 3.0 * square + 3.0 * fraction + 1.0) / 6.0,
        cube / 6.0,
    )


TABLE = [cubic((phase + 0.5) / 4.0) for phase in range(4)]
EVEN = [TABLE[p][0] + TABLE[p][3] for p in range(2)]
ODD_OUT = [TABLE[p][0] - TABLE[p][3] for p in range(2)]
ODD_IN = [TABLE[p][1] - TABLE[p][2] for p in range(2)]


def expand4(x):
    inner = x[1] + x[2]
    lift = (x[0] + x[3]) - inner
    far = x[0] - x[3]
    near = x[1] - x[2]
    even = [inner + EVEN[p] * lift for p in range(2)]
    odd = [ODD_OUT[p] * far + ODD_IN[p] * near for p in range(2)]
    return [even[0] + odd[0], even[1] + odd[1], even[1] - odd[1], even[0] - odd[0]]


def reduce4(y):
    e0, o0 = y[0] + y[3], y[0] - y[3]
    e1, o1 = y[1] + y[2], y[1] - y[2]
    outer = EVEN[0] * e0 + EVEN[1] * e1
    inner = (e0 + e1) - outer
    far = ODD_OUT[0] * o0 + ODD_OUT[1] * o1
    near = ODD_IN[0] * o0 + ODD_IN[1] * o1
    return [outer + far, inner + near, inner - near, outer - far]


S_, R0, W0, Z0, R1, W1, Q1 = range(7)


def kernel(nr, nc, elev, start, x_out, r_out, ev, tr, sx, vec, cols, fold, wts, perm, permh, one, two,
           hs, hr, ls, s1s, s1r, s2s, s2r):
    my_r, my_c = lax.axis_index("row"), lax.axis_index("col")
    rows, width = start.shape
    span = 4 * rows
    tiles = (rows + 2 * PAD) // 8
    own_t = (PAD // 8, (PAD + rows) // 8)

    def wrap(i, n):
        return lax.rem(i + n, n)

    barrier = pltpu.get_barrier_semaphore()

    def greet(r, c):
        pl.semaphore_signal(barrier, inc=1, device_id=(r, c), device_id_type=MESH)

    near = [(dr, dc) for dr in (-1, 0, 1) for dc in (-1, 0, 1) if (dr, dc) != (0, 0)]
    for dr, dc in near:
        if dr and dc:
            greet(wrap(my_r + dr, nr), wrap(my_c + dc, nc))

    def greet_col(d, carry):
        greet(my_r, lax.rem(my_c + d, nc))
        return carry

    def greet_row(d, carry):
        greet(lax.rem(my_r + d, nr), my_c)
        return carry

    lax.fori_loop(1, nc, greet_col, 0)
    lax.fori_loop(1, nr, greet_row, 0)

    own_rows = pl.ds(4 * PAD, span)
    own_el = pltpu.make_async_copy(elev, ev.at[own_rows, pl.ds(0, 4 * width)], ls.at[0])
    own_el.start()
    own_s = pltpu.make_async_copy(start, sx.at[pl.ds(PAD, rows), pl.ds(0, width)], ls.at[1])
    own_s.start()

    n_i = lax.broadcasted_iota(jnp.int32, (512, 128), 0)
    m_i = lax.broadcasted_iota(jnp.int32, (512, 128), 1)
    for q in range(4):
        perm[:, 128 * q:128 * (q + 1)] = jnp.where(n_i == 4 * m_i + q, 1.0, 0.0).astype(BF16)
    n_h = lax.broadcasted_iota(jnp.int32, (256, 128), 0)
    m_h = lax.broadcasted_iota(jnp.int32, (256, 128), 1)
    for q in range(4):
        hit = ((m_h < 32) & (n_h == 4 * m_h + q)) | ((m_h >= 96) & (n_h == 4 * m_h - 256 + q))
        permh[:, 128 * q:128 * (q + 1)] = jnp.where(hit, 1.0, 0.0).astype(BF16)
    zero = jnp.zeros((8, LANES), F32)
    for j in range(3):
        for q in range(4):
            cols[q, j, 8 * tiles:8 * tiles + 8, :] = zero
        for k in range(16):
            fold[k, j, 0:8, :] = zero

    pl.semaphore_wait(barrier, (nr - 1) + (nc - 1) + 4)

    up, down = 48, 40
    el_from_r = {1: (span - up, up), -1: (0, down), 0: (0, span)}
    el_to_r = {1: 4 * PAD - up, -1: 4 * PAD + span, 0: 4 * PAD}
    el_from_c = {1: (4 * width - LANES, LANES), -1: (0, LANES), 0: (0, 4 * width)}
    el_to_c = {1: 4 * width + LANES, -1: 4 * width, 0: 0}
    s_from_r = {1: (rows - PAD, PAD), -1: (0, PAD), 0: (0, rows)}
    s_to_r = {1: 0, -1: PAD + rows, 0: PAD}
    s_from_c = {1: (width - LANES, LANES), -1: (0, LANES), 0: (0, width)}
    s_to_c = {1: width + LANES, -1: width, 0: 0}
    sends = []
    for k, (dr, dc) in enumerate(near):
        for which, (src, dst, fr, tor, fc, toc) in enumerate(
            ((start, sx, s_from_r, s_to_r, s_from_c, s_to_c), (elev, ev, el_from_r, el_to_r, el_from_c, el_to_c))
        ):
            (r0, rn), (c0, cn) = fr[dr], fc[dc]
            sends.append(pltpu.make_async_remote_copy(
                src_ref=src.at[pl.ds(r0, rn), pl.ds(c0, cn)],
                dst_ref=dst.at[pl.ds(tor[dr], rn), pl.ds(toc[dc], cn)],
                send_sem=hs.at[2 * k + which], recv_sem=hr.at[2 * k + which],
                device_id=(wrap(my_r + dr, nr), wrap(my_c + dc, nc)), device_id_type=MESH))
    for copy in sends:
        copy.start()

    def gather(r0, rn, c0, cn, matrix, j):
        x = ev[pl.ds(r0, rn), pl.ds(c0, cn)]
        hi = x.astype(BF16)
        rest = x - hi.astype(F32)
        mid = rest.astype(BF16)
        low = (rest - mid.astype(F32)).astype(BF16)
        m = matrix[...]
        y = jnp.dot(hi, m, preferred_element_type=F32) + jnp.dot(mid, m, preferred_element_type=F32)
        y = y + jnp.dot(low, m, preferred_element_type=F32)
        for q in range(4):
            tr[3 * q + j, pl.ds(r0, rn), :] = y[:, 128 * q:128 * (q + 1)]

    own_el.wait()

    def gather_own(b, carry):
        r0 = pl.multiple_of(4 * PAD + 128 * b, 64)
        for j in range(2):
            gather(r0, 128, 512 * j, 512, perm, j)
        return carry

    lax.fori_loop(0, span // 128, gather_own, 0)
    own_s.wait()
    for copy in sends:
        copy.wait_recv()
    for j in range(2):
        gather(0, 4 * PAD, 512 * j, 512, perm, j)
        gather(4 * PAD + span, 64, 512 * j, 512, perm, j)

    def gather_side(b, carry):
        gather(pl.multiple_of(128 * b, 128), 128, 4 * width, 256, permh, 2)
        return carry

    lax.fori_loop(0, 5, gather_side, 0)

    lane = lax.broadcasted_iota(jnp.int32, (8, LANES), 1)
    sub = lax.broadcasted_iota(jnp.int32, (8, LANES), 0)
    has_left = jnp.where(my_c > 0, 1, 0)
    has_right = jnp.where(my_c < nc - 1, 1, 0)
    side = jnp.where(lane < 64, has_right, has_left) > 0
    side_f = jnp.where(side, 1.0, 0.0)
    cell_side = ((lane < 9) & (has_right > 0)) | ((lane >= 116) & (has_left > 0))

    def inside_rows(t):
        g = rows * my_r + 8 * t - PAD + sub
        return (g >= 0) & (g < nr * rows)

    def left_shift(u, c):
        r = [pltpu.roll(x, LANES - c, 1) for x in u]
        return [jnp.where(lane < LANES - c, r[j], r[(j + 1) % 3]) for j in range(3)]

    def right_shift(u, c):
        r = [pltpu.roll(x, c, 1) for x in u]
        return [jnp.where(lane < c, r[(j - 1) % 3], r[j]) for j in range(3)]

    def at(t, off=0):
        return pl.ds(pl.multiple_of(8 * t, 8) + off, 8)

    def spread(v, t):
        x = [v] + [left_shift(v, c) for c in range(1, 4)]
        for j in range(3):
            u = expand4([x[c][j] for c in range(4)])
            for q in range(4):
                cols[q, j, at(t), :] = u[q]

    def load(slot, t):
        return [vec[slot, j, at(t), :] for j in range(3)]

    def first(t, carry):
        keep = inside_rows(t)
        parts = [sx[at(t), 0:128], sx[at(t), 128:256], jnp.where(lane < 64, sx[at(t), 256:384], sx[at(t), 384:512])]
        ok = [keep, keep, keep & side]
        v = [jnp.where(ok[j], parts[j], 0.0) for j in range(3)]
        for j in range(3):
            vec[S_, j, at(t), :] = v[j]
        spread(v, t)
        return carry

    lax.fori_loop(0, tiles, first, 0)

    def rows_first(t, carry):
        i = 8 * t + sub
        okr = inside_rows(t) & (i >= PAD - 12) & (i < PAD + rows + 9)
        for j in range(3):
            ok = okr & cell_side if j == 2 else okr
            for q in range(4):
                z = expand4([cols[q, j, at(t, a), :] for a in range(4)])
                y = []
                for p in range(4):
                    el = tr[3 * q + j, pl.ds(pl.multiple_of(32 * t, 32) + p, 8, stride=4), :]
                    misfit = el - 0.25 * z[p]
                    w = huber_delta / jnp.maximum(jnp.abs(misfit), huber_delta)
                    wts[4 * p + q, j, at(t), :] = jnp.where(ok, w * 0.0625, 0.0)
                    y.append(jnp.where(ok, w * misfit * 0.25, 0.0))
                f = reduce4(y)
                for a in range(4):
                    fold[4 * a + q, j, at(t, 8), :] = f[a]
        return carry

    def rows_next(t, carry):
        for j in range(3):
            for q in range(4):
                z = expand4([cols[q, j, at(t, a), :] for a in range(4)])
                f = reduce4([z[p] * wts[4 * p + q, j, at(t), :] for p in range(4)])
                for a in range(4):
                    fold[4 * a + q, j, at(t, 8), :] = f[a]
        return carry

    def collect(t):
        g = []
        for j in range(3):
            h = []
            for q in range(4):
                parts = [fold[4 * a + q, j, at(t, 8 - a), :] for a in range(4)]
                h.append((parts[0] + parts[1]) + (parts[2] + parts[3]))
            g.append(reduce4(h))
        out = [g[j][0] for j in range(3)]
        for c in range(1, 4):
            moved = right_shift([g[j][c] for j in range(3)], c)
            out = [out[j] + moved[j] for j in range(3)]
        rowm = jnp.where(inside_rows(t), 1.0, 0.0)
        return [out[0] * rowm, out[1] * rowm, out[2] * (rowm * side_f)]

    def finish(src, dst, scale, on):
        def body(t, carry):
            out, v = collect(t), load(src, t)
            new = [out[j] + scale * v[j] for j in range(3)]
            for j in range(3):
                vec[dst, j, at(t), :] = new[j]
            if on:
                spread(new, t)
            return carry
        return body

    def sum_begin(n, accs):
        for k, acc in enumerate(accs):
            one[n, my_c, k:k + 1, :] = jnp.sum(acc, axis=0, keepdims=True)
        if len(accs) < 8:
            one[n, my_c, len(accs):8, :] = jnp.zeros((8 - len(accs), LANES), F32)

        def send(d, carry):
            pltpu.make_async_remote_copy(
                src_ref=one.at[n, my_c], dst_ref=one.at[n, my_c], send_sem=s1s.at[n, d], recv_sem=s1r.at[n, my_c],
                device_id=(my_r, lax.rem(my_c + d, nc)), device_id_type=MESH).start()
            return carry
        lax.fori_loop(1, nc, send, 0)

    def arrive(buf, send_sem, recv_sem, n, me, count, target):
        def body(d, carry):
            src = lax.rem(me + d, count)
            pltpu.make_async_remote_copy(
                src_ref=buf.at[n, src], dst_ref=buf.at[n, src], send_sem=send_sem.at[n, d],
                recv_sem=recv_sem.at[n, src], device_id=target(src), device_id_type=MESH).wait_recv()
            return carry
        lax.fori_loop(1, count, body, 0)
        parts = [buf[n, k] for k in range(count)]
        while len(parts) > 1:
            parts = [parts[k] + parts[k + 1] for k in range(0, len(parts), 2)]
        return parts[0]

    def sum_middle(n):
        two[n, my_r] = arrive(one, s1s, s1r, n, my_c, nc, lambda s: (my_r, s))

        def send(d, carry):
            pltpu.make_async_remote_copy(
                src_ref=two.at[n, my_r], dst_ref=two.at[n, my_r], send_sem=s2s.at[n, d], recv_sem=s2r.at[n, my_r],
                device_id=(lax.rem(my_r + d, nr), my_c), device_id_type=MESH).start()
            return carry
        lax.fori_loop(1, nr, send, 0)

    def sum_end(n, count):
        total = arrive(two, s2s, s2r, n, my_r, nr, lambda s: (s, my_c))
        total = jnp.broadcast_to(jnp.sum(total, axis=1, keepdims=True), (8, LANES))
        return [total[k:k + 1, :] for k in range(count)]

    def drain(n):
        def body1(d, carry):
            pltpu.make_async_remote_copy(
                src_ref=one.at[n, my_c], dst_ref=one.at[n, my_c], send_sem=s1s.at[n, d], recv_sem=s1r.at[n, my_c],
                device_id=(my_r, lax.rem(my_c + d, nc)), device_id_type=MESH).wait_send()
            return carry

        def body2(d, carry):
            pltpu.make_async_remote_copy(
                src_ref=two.at[n, my_r], dst_ref=two.at[n, my_r], send_sem=s2s.at[n, d], recv_sem=s2r.at[n, my_r],
                device_id=(lax.rem(my_r + d, nr), my_c), device_id_type=MESH).wait_send()
            return carry
        lax.fori_loop(1, nc, body1, 0)
        lax.fori_loop(1, nr, body2, 0)

    def dots(products, count):
        def body(t, accs):
            for j in range(2):
                accs = tuple(a + p for a, p in zip(accs, products(j, t)))
            return accs
        return lax.fori_loop(own_t[0], own_t[1], body, (zero,) * count)

    def get(slot, j, t):
        return vec[slot, j, at(t), :]

    lax.fori_loop(0, 20, rows_first, 0)
    lax.fori_loop(0, 20, finish(S_, R0, -ridge, True), 0)
    lax.fori_loop(0, 19, rows_next, 0)
    lax.fori_loop(1, 19, finish(R0, W0, ridge, True), 0)

    def products0(j, t):
        r, w = get(R0, j, t), get(W0, j, t)
        return r * r, r * w

    sum_begin(0, dots(products0, 2))
    lax.fori_loop(1, 19, rows_next, 0)
    sum_middle(0)
    lax.fori_loop(1, 19, finish(W0, Z0, ridge, False), 0)
    rr0, r0w0 = sum_end(0, 2)
    alpha0 = rr0 / r0w0

    def step1(t, carry):
        r, w, z = load(R0, t), load(W0, t), load(Z0, t)
        r1 = [r[j] - alpha0 * w[j] for j in range(3)]
        w1 = [w[j] - alpha0 * z[j] for j in range(3)]
        for j in range(3):
            vec[R1, j, at(t), :] = r1[j]
            vec[W1, j, at(t), :] = w1[j]
        spread(w1, t)
        return carry

    lax.fori_loop(1, 19, step1, 0)

    def products1(j, t):
        r1, w1, w0 = get(R1, j, t), get(W1, j, t), get(W0, j, t)
        return r1 * r1, r1 * w1, r1 * w0

    sum_begin(1, dots(products1, 3))
    lax.fori_loop(1, 18, rows_next, 0)
    sum_middle(1)
    lax.fori_loop(2, 18, finish(W1, Q1, ridge, False), 0)
    rr1, r1w1, r1w0 = sum_end(1, 3)
    beta0 = rr1 / rr0
    d1s1 = r1w1 + beta0 * (2.0 * r1w0 + beta0 * r0w0)
    alpha1 = rr1 / d1s1

    def products2(j, t):
        r0, w0, z0 = get(R0, j, t), get(W0, j, t), get(Z0, j, t)
        r1, w1, q1 = get(R1, j, t), get(W1, j, t), get(Q1, j, t)
        d1 = r1 + beta0 * r0
        s1 = w1 + beta0 * w0
        z1 = q1 + beta0 * z0
        r2 = r1 - alpha1 * s1
        w2 = w1 - alpha1 * z1
        x1 = get(S_, j, t) + alpha0 * r0 + alpha1 * d1
        vec[R0, j, at(t), :] = d1
        vec[S_, j, at(t), :] = x1
        vec[R1, j, at(t), :] = r2
        vec[W1, j, at(t), :] = s1
        vec[Q1, j, at(t), :] = w2
        return r2 * r2, r2 * w2, r2 * s1

    sum_begin(2, dots(products2, 3))
    sum_middle(2)
    rr2, r2w2, r2s1 = sum_end(2, 3)
    beta1 = rr2 / rr1
    alpha2 = rr2 / (r2w2 + beta1 * (2.0 * r2s1 + beta1 * d1s1))

    def last(t, carry):
        out_rows = pl.ds(pl.multiple_of(8 * t, 8) - PAD, 8)
        for j in range(2):
            r2, d1, s1, w2 = get(R1, j, t), get(R0, j, t), get(W1, j, t), get(Q1, j, t)
            x_out[out_rows, 128 * j:128 * (j + 1)] = get(S_, j, t) + alpha2 * (r2 + beta1 * d1)
            r_out[out_rows, 128 * j:128 * (j + 1)] = r2 - alpha2 * (w2 + beta1 * s1)
        return carry

    lax.fori_loop(own_t[0], own_t[1], last, 0)
    for copy in sends:
        copy.wait_send()
    for n in range(3):
        drain(n)


def solution(mesh):
    nr, nc = mesh.shape["row"], mesh.shape["col"]

    def shards(elevation, start_controls):
        rows, width = start_controls.shape
        out = jax.ShapeDtypeStruct((rows, width), F32)
        tall = rows + 2 * PAD
        return pl.pallas_call(
            functools.partial(kernel, nr, nc),
            out_shape=(out, out),
            in_specs=[pl.BlockSpec(memory_space=pl.ANY)] * 2,
            out_specs=(pl.BlockSpec(memory_space=pltpu.VMEM),) * 2,
            scratch_shapes=[
                pltpu.VMEM((4 * tall, 4 * width + 2 * LANES), F32),
                pltpu.VMEM((12, 4 * tall, LANES), F32),
                pltpu.VMEM((tall, width + 2 * LANES), F32),
                pltpu.VMEM((7, 3, tall, LANES), F32),
                pltpu.VMEM((4, 3, tall + 8, LANES), F32),
                pltpu.VMEM((16, 3, tall + 8, LANES), F32),
                pltpu.VMEM((16, 3, tall, LANES), F32),
                pltpu.VMEM((512, 512), BF16),
                pltpu.VMEM((256, 512), BF16),
                pltpu.VMEM((3, nc, 8, LANES), F32),
                pltpu.VMEM((3, nr, 8, LANES), F32),
                pltpu.SemaphoreType.DMA((16,)),
                pltpu.SemaphoreType.DMA((16,)),
                pltpu.SemaphoreType.DMA((2,)),
                pltpu.SemaphoreType.DMA((3, nc)),
                pltpu.SemaphoreType.DMA((3, nc)),
                pltpu.SemaphoreType.DMA((3, nr)),
                pltpu.SemaphoreType.DMA((3, nr)),
            ],
            compiler_params=pltpu.CompilerParams(
                collective_id=0, has_side_effects=True, vmem_limit_bytes=50 * 1024 * 1024
            ),
        )(elevation, start_controls)

    return jax.shard_map(
        shards,
        mesh=mesh,
        in_specs=(P("row", "col"), P("row", "col")),
        out_specs=(P("row", "col"), P("row", "col")),
        check_vma=False,
    )
```

time: 676 us -> 88.5 us (0.13); the launches traced: 666 us -> 88.4 us
  blocking collectives: 406 us -> 0 us
  local copies, waits for them, and re-layouts: 117 us -> 3.8 us
  Pallas kernels: 0 us -> 84 us
  other arithmetic: 47.9 us -> 0 us
  starting transfers between devices: 44.5 us -> 0 us
  waiting for transfers between devices: 41.8 us -> 0 us
  between operations: 8.28 us -> 0.65 us
    psum x5 -> x0, blocking collectives: 406 us -> none  [the longest x3 237 us: squares(): return lax.psum(jnp.sum(residual * residual), ('row', 'col'))]
    pallas_call x0 -> x1, Pallas kernels: none -> 84 us  [shards(): pl.pallas_call(functools.partial(kernel, nr, nc), out_shape=(out, out), i...]
    ppermute x16 -> x0, starting transfers between devices: 44.5 us -> none  [from_behind(): return lax.ppermute(block, axis, route)]
    ppermute x16 -> x0, waiting for transfers between devices: 41.8 us -> none  [from_behind(): return lax.ppermute(block, axis, route)]
    unnamed x54 -> x6, local copies, waits for them, and re-layouts: 39.1 us -> 3.8 us
    reshape x16 -> x0, local copies, waits for them, and re-layouts: 32.1 us -> none  [the longest x4 11.8 us: expand_cols(): return jnp.stack(outputs, axis=2).reshape(field.shape[0], 4 * count)]
    slice x10 -> x0, local copies, waits for them, and re-layouts: 28.6 us -> none  [the longest x4 23.2 us: reduce_cols(): part = table[0][offset] * grouped[:, :, 0]]
    add x27 -> x0, other arithmetic: 18.1 us -> none  [the longest x4 5.88 us: reduce_cols(): part = part + table[phase][offset] * grouped[:, :, phase]]
  transfers between devices with their start and end apart: 16 -> 0, of which waited for: 15 -> 0; matrix products, arithmetic and copies ran while one was open for 1% -> 0% of each run, Pallas kernels for 0% -> 0%
where the time goes in v1:
time: 88.5 us; the launch traced here: 88.4 us
  Pallas kernels  84 us (95%)
  local copies, waits for them, and re-layouts  3.8 us (4%)
    pallas_call x1, Pallas kernels, shards(): pl.pallas_call(functools.partial(kernel, nr, nc), out_shape=(out, out), i...  84 us
    unnamed x6, local copies, waits for them, and re-layouts  3.8 us

profile of v1, /device:TPU:1, one launch (start us, length us, event | category | flops | bytes accessed | tf_op | source)
XLA Modules:
  0.0 88.4 jit_solution(8056083853798864438)
XLA Ops:
  0.6 0.0 copy-start
  0.6 1.6 %copy-done = f32[512,1024]{1,0:T(8,128)S(1)} copy-done((f32[512,1024]{1,0:T(8,128)S(1)}, f32[512,1024]{1,0:T(8,128)}, u32[]{:S(2)}) %copy-start) | copy-done | bytes 2097176
  2.2 0.0 copy-start.1
  2.2 0.9 %copy-done.1 = f32[128,256]{1,0:T(8,128)S(1)} copy-done((f32[128,256]{1,0:T(8,128)S(1)}, f32[128,256]{1,0:T(8,128)}, u32[]{:S(2)}) %copy-start.1) | copy-done | bytes 131096
  3.1 84.0 %shard_map.41 = (f32[128,256]{1,0:T(8,128)S(1)}, f32[128,256]{1,0:T(8,128)S(1)}) custom-call(f32[512,1024]{1,0:T(8,128)S(1)} %copy-done, f32[128,256]{1,0:T(8,128)S(1)} %copy-done.1), custom_call_target="tpu_custom_call" | custom-call | tf_op jit(solution)/shard_map/pallas_call | solution.py:424
  87.1 0.7 copy.6
  87.8 0.7 copy.7
Async XLA Ops:
  0.6 1.6 %copy-start = (f32[512,1024]{1,0:T(8,128)S(1)}, f32[512,1024]{1,0:T(8,128)}, u32[]{:S(2)}) copy-start(f32[512,1024]{1,0:T(8,128)} %elev.1) | copy-start | bytes 6291460
  2.2 0.9 %copy-start.1 = (f32[128,256]{1,0:T(8,128)S(1)}, f32[128,256]{1,0:T(8,128)}, u32[]{:S(2)}) copy-start(f32[128,256]{1,0:T(8,128)} %start.1) | copy-start | bytes 393220

commit v2 on v0

--- a/solution.py
+++ b/solution.py
@@ -1,19 +1,23 @@
+import functools
+
 import jax
 import jax.numpy as jnp
 from jax import lax
+from jax.experimental import pallas as pl
+from jax.experimental.pallas import tpu as pltpu
 from jax.sharding import PartitionSpec as P
 
-ITERS = 3
-
-
+MESH = pl.DeviceIdType.MESH
+F32 = jnp.float32
+BF16 = jnp.bfloat16
 huber_delta = 1.5
 ridge = 0.25
-
-
-def from_behind(block, axis, distance):
-    devices = range(lax.axis_size(axis))
-    route = [(i - distance, i) for i in devices if i - distance in devices]
-    return lax.ppermute(block, axis, route)
+ITERS = 3
+SHIFT = 5.0
+AMPLIFY = 400.0
+
+PAD = 16
+LANES = 128
 
 
 def cubic(fraction):
@@ -28,8 +32,391 @@
     )
 
 
-def spline_table():
-    return [list(cubic((phase + 0.5) / 4.0)) for phase in range(4)]
+TABLE = [cubic((phase + 0.5) / 4.0) for phase in range(4)]
+EVEN = [TABLE[p][0] + TABLE[p][3] for p in range(2)]
+ODD_OUT = [TABLE[p][0] - TABLE[p][3] for p in range(2)]
+ODD_IN = [TABLE[p][1] - TABLE[p][2] for p in range(2)]
+
+
+def expand4(x):
+    inner = x[1] + x[2]
+    lift = (x[0] + x[3]) - inner
+    far = x[0] - x[3]
+    near = x[1] - x[2]
+    even = [inner + EVEN[p] * lift for p in range(2)]
+    odd = [ODD_OUT[p] * far + ODD_IN[p] * near for p in range(2)]
+    return [even[0] + odd[0], even[1] + odd[1], even[1] - odd[1], even[0] - odd[0]]
+
+
+def reduce4(y):
+    e0, o0 = y[0] + y[3], y[0] - y[3]
+    e1, o1 = y[1] + y[2], y[1] - y[2]
+    outer = EVEN[0] * e0 + EVEN[1] * e1
+    inner = (e0 + e1) - outer
+    far = ODD_OUT[0] * o0 + ODD_OUT[1] * o1
+    near = ODD_IN[0] * o0 + ODD_IN[1] * o1
+    return [outer + far, inner + near, inner - near, outer - far]
+
+
+def cg_scalars(nu):
+    worst = []
+
+    def form(p, q):
+        total, size = None, None
+        for i, a in enumerate(p):
+            for j, b in enumerate(q):
+                m, bound = nu[i + j]
+                term = (a * b) * m
+                big = jnp.abs(a * b) * bound
+                total = term if total is None else total + term
+                size = big if size is None else size + big
+        worst.append(size / total)
+        return total
+
+    def operate(p):
+        q = [SHIFT * a for a in p] + [p[-1]]
+        for i in range(1, len(p)):
+            q[i] = q[i] + p[i - 1]
+        return q
+
+    one = jnp.ones_like(nu[0][0])
+    residual, direction = [one], [one]
+    step = [None] * ITERS
+    norm_now = nu[0][0]
+    for k in range(ITERS):
+        image = operate(direction)
+        alpha = norm_now / form(direction, image)
+        for i, d in enumerate(direction):
+            step[i] = alpha * d if step[i] is None else step[i] + alpha * d
+        residual = [residual[i] - alpha * image[i] if i < k + 1 else -(alpha * image[i]) for i in range(k + 2)]
+        if k < ITERS - 1:
+            norm_next = form(residual, residual)
+            beta = norm_next / norm_now
+            direction = [residual[i] + beta * direction[i] if i < k + 1 else residual[i] for i in range(k + 2)]
+            norm_now = norm_next
+    fine = one
+    for w in worst:
+        fine = jnp.where((w > 0.0) & (w < AMPLIFY), fine, 0.0)
+    return step, residual, fine
+
+
+def loop(low, high, step, body):
+    def trip(k, carry):
+        body([low + step * k + i for i in range(step)])
+        return carry
+    lax.fori_loop(0, (high - low) // step, trip, 0)
+
+
+def kernel(nr, nc, elev, start, x_out, r_out, flag, ev, tr, sx, side, side_t, sent, got, sent_s, got_s, cols, fold, wts,
+           s_v, v0, v1, v2, v3, perm, permh, permt, one, two, hs, hr, ls, s1s, s1r, s2s, s2r):
+    my_r, my_c = lax.axis_index("row"), lax.axis_index("col")
+    rows, width = start.shape
+    span = 4 * rows
+    tiles = (rows + 2 * PAD) // 8
+    own_low, own_high = PAD // 8, (PAD + rows) // 8
+
+    def wrap(i, n):
+        return lax.rem(i + n, n)
+
+    barrier = pltpu.get_barrier_semaphore()
+
+    def greet(r, c):
+        pl.semaphore_signal(barrier, inc=1, device_id=(r, c), device_id_type=MESH)
+
+    near = [(dr, dc) for dr in (-1, 0, 1) for dc in (-1, 0, 1) if (dr, dc) != (0, 0)]
+    for dr, dc in near:
+        if dr and dc:
+            greet(wrap(my_r + dr, nr), wrap(my_c + dc, nc))
+    for d in range(1, nc):
+        greet(my_r, lax.rem(my_c + d, nc))
+    for d in range(1, nr):
+        greet(lax.rem(my_r + d, nr), my_c)
+
+    own_el = pltpu.make_async_copy(elev, ev.at[pl.ds(4 * PAD, span), pl.ds(0, 4 * width)], ls.at[0])
+    own_el.start()
+    own_s = pltpu.make_async_copy(start, sx.at[pl.ds(PAD, rows), pl.ds(0, width)], ls.at[1])
+    own_s.start()
+
+    n_i = lax.broadcasted_iota(jnp.int32, (512, 128), 0)
+    m_i = lax.broadcasted_iota(jnp.int32, (512, 128), 1)
+    for q in range(4):
+        perm[:, 128 * q:128 * (q + 1)] = jnp.where(n_i == 4 * m_i + q, 1.0, 0.0).astype(BF16)
+    n_h = lax.broadcasted_iota(jnp.int32, (256, 128), 0)
+    m_h = lax.broadcasted_iota(jnp.int32, (256, 128), 1)
+    for q in range(4):
+        hit = ((m_h < 32) & (n_h == 4 * m_h + q)) | ((m_h >= 96) & (n_h == 4 * m_h - 256 + q))
+        permh[:, 128 * q:128 * (q + 1)] = jnp.where(hit, 1.0, 0.0).astype(BF16)
+    n_t = lax.broadcasted_iota(jnp.int32, (128, 128), 0)
+    m_t = lax.broadcasted_iota(jnp.int32, (128, 128), 1)
+    for q in range(4):
+        hit = ((n_t < 48) & (n_t == 4 * m_t + q)) | ((n_t >= 48) & (n_t == 4 * m_t - 416 + q) & (n_t < 96))
+        permt[:, 128 * q:128 * (q + 1)] = jnp.where(hit, 1.0, 0.0).astype(BF16)
+    zero = jnp.zeros((8, LANES), F32)
+    for j in range(3):
+        for q in range(4):
+            cols[q, j, 8 * tiles:8 * tiles + 8, :] = zero
+        for k in range(16):
+            fold[k, j, 0:8, :] = zero
+    got_s[16:112, :] = jnp.zeros((96, rows), F32)
+    got[96:128, :] = jnp.zeros((32, span), F32)
+
+    def gather(x, matrix, j, r0, rn):
+        hi = x.astype(BF16)
+        rest = x - hi.astype(F32)
+        mid = rest.astype(BF16)
+        low = (rest - mid.astype(F32)).astype(BF16)
+        m = matrix[...]
+        y = jnp.dot(hi, m, preferred_element_type=F32) + jnp.dot(mid, m, preferred_element_type=F32)
+        y = y + jnp.dot(low, m, preferred_element_type=F32)
+        for q in range(4):
+            tr[3 * q + j, pl.ds(r0, rn), :] = y[:, 128 * q:128 * (q + 1)]
+
+    def gather_own(b, carry):
+        r0 = pl.multiple_of(4 * PAD + 128 * b, 64)
+        for j in range(2):
+            gather(ev[pl.ds(r0, 128), pl.ds(512 * j, 512)], perm, j, r0, 128)
+        return carry
+
+    own_el.wait()
+    own_s.wait()
+    for b in range(span // 128):
+        block = ev[4 * PAD + 128 * b:4 * PAD + 128 * (b + 1), :]
+        sent[0:48, 128 * b:128 * (b + 1)] = block[:, 0:128].T[0:48]
+        sent[48:96, 128 * b:128 * (b + 1)] = block[:, 4 * width - 128:4 * width].T[80:128]
+    sent_s[0:16, :] = sx[PAD:PAD + rows, 0:128].T[0:16]
+    sent_s[16:32, :] = sx[PAD:PAD + rows, width - 128:width].T[112:128]
+    lax.fori_loop(0, span // 128, gather_own, 0)
+
+    pl.semaphore_wait(barrier, (nr - 1) + (nc - 1) + 4)
+
+    up, down = 48, 40
+    el_from_r = {1: (span - up, up), -1: (0, down)}
+    el_to_r = {1: 4 * PAD - up, -1: 4 * PAD + span}
+    el_from_c = {1: (4 * width - LANES, LANES), -1: (0, LANES), 0: (0, 4 * width)}
+    el_to_c = {1: 4 * width + LANES, -1: 4 * width, 0: 0}
+    s_from_r = {1: (rows - PAD, PAD), -1: (0, PAD)}
+    s_to_r = {1: 0, -1: PAD + rows}
+    s_from_c = {1: (width - LANES, LANES), -1: (0, LANES), 0: (0, width)}
+    s_to_c = {1: width + LANES, -1: width, 0: 0}
+    sends = []
+
+    def send_to(dr, dc, src, dst):
+        k = len(sends)
+        sends.append(pltpu.make_async_remote_copy(
+            src_ref=src, dst_ref=dst, send_sem=hs.at[k], recv_sem=hr.at[k],
+            device_id=(wrap(my_r + dr, nr), wrap(my_c + dc, nc)), device_id_type=MESH))
+        sends[-1].start()
+
+    for dr, dc in sorted(near, key=lambda o: (o[0] == 0, o[1] != 0)):
+        if dr:
+            for src, dst, fr, tor, fc, toc in ((elev, ev, el_from_r, el_to_r, el_from_c, el_to_c),
+                                               (start, sx, s_from_r, s_to_r, s_from_c, s_to_c)):
+                (r0, rn), (c0, cn) = fr[dr], fc[dc]
+                send_to(dr, dc, src.at[pl.ds(r0, rn), pl.ds(c0, cn)], dst.at[pl.ds(tor[dr], rn), pl.ds(toc[dc], cn)])
+        else:
+            part, to_s = (pl.ds(0, 48), pl.ds(0, 16)) if dc < 0 else (pl.ds(48, 48), pl.ds(112, 16))
+            send_to(dr, dc, sent.at[part], got.at[part])
+            send_to(dr, dc, sent_s.at[pl.ds(0, 16) if dc < 0 else pl.ds(16, 16)], got_s.at[to_s])
+
+    for copy in sends:
+        copy.wait_recv()
+    for r0 in (0, 4 * PAD + span):
+        for j in range(2):
+            gather(ev[r0:r0 + 64, 512 * j:512 * (j + 1)], perm, j, r0, 64)
+        gather(ev[r0:r0 + 64, 4 * width:4 * width + 256], permh, 2, r0, 64)
+    for b in range(span // 128):
+        gather(got[:, 128 * b:128 * (b + 1)].T, permt, 2, 4 * PAD + 128 * b, 128)
+
+    lane = lax.broadcasted_iota(jnp.int32, (8, LANES), 1)
+    sub = lax.broadcasted_iota(jnp.int32, (8, LANES), 0)
+    has_left = jnp.where(my_c > 0, 1, 0)
+    has_right = jnp.where(my_c < nc - 1, 1, 0)
+    beside = jnp.where(lane < 64, has_right, has_left) > 0
+    beside_f = jnp.where(beside, 1.0, 0.0)
+    cell_side = ((lane < 9) & (has_right > 0)) | ((lane >= 116) & (has_left > 0))
+
+    side[PAD:PAD + rows, :] = got_s[...].T
+    lane2 = lax.broadcasted_iota(jnp.int32, (PAD, LANES), 1)
+    for r0 in (0, PAD + rows):
+        side[r0:r0 + PAD, :] = jnp.where(
+            lane2 < 64, sx[r0:r0 + PAD, width:width + LANES], sx[r0:r0 + PAD, width + LANES:width + 2 * LANES])
+
+    def inside_rows(t):
+        g = rows * my_r + 8 * t - PAD + sub
+        return (g >= 0) & (g < nr * rows)
+
+    def left_shift(u, c):
+        r = [pltpu.roll(x, LANES - c, 1) for x in u]
+        return [jnp.where(lane < LANES - c, r[j], r[(j + 1) % 3]) for j in range(3)]
+
+    def right_shift(u, c):
+        r = [pltpu.roll(x, c, 1) for x in u]
+        return [jnp.where(lane < c, r[(j - 1) % 3], r[j]) for j in range(3)]
+
+    def at(t, off=0):
+        return pl.ds(pl.multiple_of(8 * t, 8) + off, 8)
+
+    def spread(v):
+        x = [v] + [left_shift(v, c) for c in range(1, 4)]
+        return [expand4([x[c][j] for c in range(4)]) for j in range(3)]
+
+    def keep_spread(u, t):
+        for j in range(3):
+            for q in range(4):
+                cols[q, j, at(t), :] = u[j][q]
+
+    def first(ts):
+        done = []
+        for t in ts:
+            keep = inside_rows(t)
+            parts = [sx[at(t), 0:128], sx[at(t), 128:256], side[at(t), :]]
+            ok = [keep, keep, keep & beside]
+            v = [jnp.where(ok[j], parts[j], 0.0) for j in range(3)]
+            done.append((t, v, spread(v)))
+        for t, v, u in done:
+            for j in range(3):
+                s_v[j, at(t), :] = v[j]
+            keep_spread(u, t)
+
+    def rows_first(ts):
+        for t in ts:
+            i = 8 * t + sub
+            okr = inside_rows(t) & (i >= PAD - 12) & (i < PAD + rows + 9)
+            for j in range(3):
+                ok = okr & cell_side if j == 2 else okr
+                for q in range(4):
+                    z = expand4([cols[q, j, at(t, a), :] for a in range(4)])
+                    y = []
+                    for p in range(4):
+                        el = tr[3 * q + j, pl.ds(pl.multiple_of(32 * t, 32) + p, 8, stride=4), :]
+                        misfit = el - 0.25 * z[p]
+                        w = huber_delta / jnp.maximum(jnp.abs(misfit), huber_delta)
+                        wts[4 * p + q, j, at(t), :] = jnp.where(ok, w * 0.0625, 0.0)
+                        y.append(jnp.where(ok, w * misfit * 0.25, 0.0))
+                    f = reduce4(y)
+                    for a in range(4):
+                        fold[4 * a + q, j, at(t, 8), :] = f[a]
+
+    def rows_next(ts):
+        for t in ts:
+            for j in range(3):
+                for q in range(4):
+                    z = expand4([cols[q, j, at(t, a), :] for a in range(4)])
+                    f = reduce4([z[p] * wts[4 * p + q, j, at(t), :] for p in range(4)])
+                    for a in range(4):
+                        fold[4 * a + q, j, at(t, 8), :] = f[a]
+
+    def collect(t):
+        g = []
+        for j in range(3):
+            h = []
+            for q in range(4):
+                parts = [fold[4 * a + q, j, at(t, 8 - a), :] for a in range(4)]
+                h.append((parts[0] + parts[1]) + (parts[2] + parts[3]))
+            g.append(reduce4(h))
+        out = [g[j][0] for j in range(3)]
+        for c in range(1, 4):
+            moved = right_shift([g[j][c] for j in range(3)], c)
+            out = [out[j] + moved[j] for j in range(3)]
+        rowm = jnp.where(inside_rows(t), 1.0, 0.0)
+        return [out[0] * rowm, out[1] * rowm, out[2] * (rowm * beside_f)]
+
+    def finish(src, dst, scale, on):
+        def body(ts):
+            done = []
+            for t in ts:
+                out = collect(t)
+                new = [out[j] + scale * src[j, at(t), :] for j in range(3)]
+                done.append((t, new, spread(new) if on else None))
+            for t, new, u in done:
+                for j in range(3):
+                    dst[j, at(t), :] = new[j]
+                if on:
+                    keep_spread(u, t)
+        return body
+
+    loop(0, 20, 2, first)
+    loop(0, 20, 1, rows_first)
+    loop(0, 20, UF, finish(s_v, v0, -ridge, True))
+    loop(0, 19, 1, rows_next)
+    loop(1, 19, UF1, finish(v0, v1, ridge - SHIFT, True))
+    loop(1, 19, 1, rows_next)
+    loop(1, 19, UF1, finish(v1, v2, ridge - SHIFT, True))
+
+    def moments(t, accs):
+        for j in range(2):
+            a, b, c = v0[j, at(t), :], v1[j, at(t), :], v2[j, at(t), :]
+            energy = None
+            for q in range(4):
+                z = expand4([cols[q, j, at(t, k), :] for k in range(4)])
+                for p in range(4):
+                    e = z[p] * z[p] * wts[4 * p + q, j, at(t), :]
+                    energy = e if energy is None else energy + e
+            accs = tuple(x + y for x, y in zip(accs, (a * a, a * b, b * b, b * c, c * c, energy)))
+        return accs
+
+    accs = lax.fori_loop(own_low, own_high, moments, (zero,) * 6)
+
+    for k, acc in enumerate(accs):
+        one[my_c, k:k + 1, :] = jnp.sum(acc, axis=0, keepdims=True)
+    one[my_c, 6:8, :] = jnp.zeros((2, LANES), F32)
+
+    def exchange(buf, send_sem, recv_sem, me, count, target):
+        copies = []
+        for d in range(1, count):
+            copies.append(pltpu.make_async_remote_copy(
+                src_ref=buf.at[me], dst_ref=buf.at[me], send_sem=send_sem.at[d], recv_sem=recv_sem.at[me],
+                device_id=target(lax.rem(me + d, count)), device_id_type=MESH))
+            copies[-1].start()
+        return copies
+
+    def arrive(buf, send_sem, recv_sem, me, count, target):
+        for d in range(1, count):
+            src = lax.rem(me + d, count)
+            pltpu.make_async_remote_copy(
+                src_ref=buf.at[src], dst_ref=buf.at[src], send_sem=send_sem.at[d], recv_sem=recv_sem.at[src],
+                device_id=target(src), device_id_type=MESH).wait_recv()
+        parts = [buf[k] for k in range(count)]
+        while len(parts) > 1:
+            parts = [parts[k] + parts[k + 1] for k in range(0, len(parts), 2)]
+        return parts[0]
+
+    sends += exchange(one, s1s, s1r, my_c, nc, lambda s: (my_r, s))
+    loop(1, 18, 1, rows_next)
+    two[my_r] = arrive(one, s1s, s1r, my_c, nc, lambda s: (my_r, s))
+    sends += exchange(two, s2s, s2r, my_r, nr, lambda s: (s, my_c))
+    loop(2, 18, UF2, finish(v2, v3, ridge - SHIFT, False))
+    total = arrive(two, s2s, s2r, my_r, nr, lambda s: (s, my_c))
+    total = jnp.broadcast_to(jnp.sum(total, axis=1, keepdims=True), (8, LANES))
+    nu = [total[k:k + 1, :] for k in range(6)]
+    pairs = [(m, jnp.abs(m)) for m in nu]
+    pairs[5] = (nu[5] + (ridge - SHIFT) * nu[4], nu[5] + SHIFT * nu[4])
+    step, last, fine = cg_scalars(pairs)
+
+    step, last = ([jnp.broadcast_to(k, (8, LANES)) for k in ks] for ks in (step, last))
+    flag[...] = jnp.broadcast_to(fine, (8, LANES))
+
+    def final(ts):
+        for t in ts:
+            out_rows = pl.ds(pl.multiple_of(8 * t, 8) - PAD, 8)
+            for j in range(2):
+                v = [ref[j, at(t), :] for ref in (v0, v1, v2, v3)]
+                x_out[out_rows, 128 * j:128 * (j + 1)] = (
+                    s_v[j, at(t), :] + ((step[0] * v[0] + step[1] * v[1]) + step[2] * v[2]))
+                r_out[out_rows, 128 * j:128 * (j + 1)] = (
+                    (last[0] * v[0] + last[1] * v[1]) + (last[2] * v[2] + last[3] * v[3]))
+
+    loop(own_low, own_high, 2, final)
+    for copy in sends:
+        copy.wait_send()
+
+
+UF, UF1, UF2 = 4, 3, 4
+
+def from_behind(block, axis, distance):
+    devices = range(lax.axis_size(axis))
+    route = [(i - distance, i) for i in devices if i - distance in devices]
+    return lax.ppermute(block, axis, route)
 
 
 def expand_rows(field, table):
@@ -100,8 +487,8 @@
     return lax.psum(jnp.sum(residual * residual), ("row", "col"))
 
 
-def shards(elevation, start_controls):
-    table = spline_table()
+def step_by_step(elevation, start_controls):
+    table = TABLE
 
     def evaluate(tile):
         return expand_cols(expand_rows(extend(tile), table), table)
@@ -128,6 +515,51 @@
 
 
 def solution(mesh):
+    nr, nc = mesh.shape["row"], mesh.shape["col"]
+
+    def shards(elevation, start_controls):
+        rows, width = start_controls.shape
+        out = jax.ShapeDtypeStruct((rows, width), F32)
+        tall = rows + 2 * PAD
+        field = pltpu.VMEM((3, tall, LANES), F32)
+        x, r, fine = pl.pallas_call(
+            functools.partial(kernel, nr, nc),
+            out_shape=(out, out, jax.ShapeDtypeStruct((8, LANES), F32)),
+            in_specs=[pl.BlockSpec(memory_space=pltpu.HBM)] * 2,
+            out_specs=(pl.BlockSpec(memory_space=pltpu.VMEM),) * 3,
+            scratch_shapes=[
+                pltpu.VMEM((4 * tall, 4 * width + 2 * LANES), F32),
+                pltpu.VMEM((12, 4 * tall, LANES), F32),
+                pltpu.VMEM((tall, width + 2 * LANES), F32),
+                pltpu.VMEM((tall, LANES), F32),
+                pltpu.VMEM((8, LANES), F32),
+                pltpu.VMEM((96, 4 * rows), F32),
+                pltpu.VMEM((128, 4 * rows), F32),
+                pltpu.VMEM((32, rows), F32),
+                pltpu.VMEM((LANES, rows), F32),
+                pltpu.VMEM((4, 3, tall + 8, LANES), F32),
+                pltpu.VMEM((16, 3, tall + 8, LANES), F32),
+                pltpu.VMEM((16, 3, tall, LANES), F32),
+                field, field, field, field, field,
+                pltpu.VMEM((512, 512), BF16),
+                pltpu.VMEM((256, 512), BF16),
+                pltpu.VMEM((128, 512), BF16),
+                pltpu.VMEM((nc, 8, LANES), F32),
+                pltpu.VMEM((nr, 8, LANES), F32),
+                pltpu.SemaphoreType.DMA((16,)),
+                pltpu.SemaphoreType.DMA((16,)),
+                pltpu.SemaphoreType.DMA((2,)),
+                pltpu.SemaphoreType.DMA((nc,)),
+                pltpu.SemaphoreType.DMA((nc,)),
+                pltpu.SemaphoreType.DMA((nr,)),
+                pltpu.SemaphoreType.DMA((nr,)),
+            ],
+            compiler_params=pltpu.CompilerParams(
+                collective_id=0, has_side_effects=True, vmem_limit_bytes=50 * 1024 * 1024
+            ),
+        )(elevation, start_controls)
+        return lax.cond(fine[0, 0] > 0.5, lambda: (x, r), lambda: step_by_step(elevation, start_controls))
+
     return jax.shard_map(
         shards,
         mesh=mesh,

time: 676 us -> 58.7 us (0.09); the launches traced: 666 us -> 58.6 us
  blocking collectives: 406 us -> 0 us
  local copies, waits for them, and re-layouts: 117 us -> 3.65 us
  Pallas kernels: 0 us -> 53.4 us
  other arithmetic: 47.9 us -> 0 us
  starting transfers between devices: 44.5 us -> 0 us
  waiting for transfers between devices: 41.8 us -> 0 us
  between operations: 8.28 us -> 1.32 us
    psum x5 -> x0, blocking collectives: 406 us -> none  [the longest x3 237 us: squares(): return lax.psum(jnp.sum(residual * residual), ('row', 'col'))]
    pallas_call x0 -> x1, Pallas kernels: none -> 53.4 us  [shards(): pl.pallas_call(functools.partial(kernel, nr, nc), out_shape=(out, out, ja...]
    ppermute x16 -> x0, starting transfers between devices: 44.5 us -> none  [from_behind(): return lax.ppermute(block, axis, route)]
    ppermute x16 -> x0, waiting for transfers between devices: 41.8 us -> none  [from_behind(): return lax.ppermute(block, axis, route)]
    unnamed x54 -> x4, local copies, waits for them, and re-layouts: 39.1 us -> 3.14 us
    reshape x16 -> x0, local copies, waits for them, and re-layouts: 32.1 us -> none  [the longest x4 11.8 us: expand_cols(): return jnp.stack(outputs, axis=2).reshape(field.shape[0], 4 * count)]
    slice x10 -> x1, local copies, waits for them, and re-layouts: 28.6 us -> 0.51 us  [shards(): fine[0, 0] > 0.5]
    add x27 -> x0, other arithmetic: 18.1 us -> none  [the longest x4 5.88 us: reduce_cols(): part = part + table[phase][offset] * grouped[:, :, phase]]
  transfers between devices with their start and end apart: 16 -> 0, of which waited for: 15 -> 0; matrix products, arithmetic and copies ran while one was open for 1% -> 0% of each run, Pallas kernels for 0% -> 0%
where the time goes in v2:
time: 58.7 us; the launch traced here: 58.6 us
  Pallas kernels  53.4 us (91%)
  local copies, waits for them, and re-layouts  3.65 us (6%)
  between operations  1.32 us (2%)
    pallas_call x1, Pallas kernels, shards(): pl.pallas_call(functools.partial(kernel, nr, nc), out_shape=(out, out, ja...  53.4 us
    unnamed x4, local copies, waits for them, and re-layouts  3.14 us

profile of v2, /device:TPU:1, one launch (start us, length us, event | category | flops | bytes accessed | tf_op | source)
XLA Modules:
  0.0 58.6 jit_solution(12289740362826055790)
XLA Ops:
  0.6 0.0 copy-start.1
  0.6 53.4 %shard_map.45 = (f32[128,256]{1,0:T(8,128)}, f32[128,256]{1,0:T(8,128)}, f32[8,128]{1,0:T(8,128)S(1)}) custom-call(f32[512,1024]{1,0:T(8,128)} %elev.1, f32[128,256]{1,0:T(8,128)} %start.1), custom_call_target="tpu_custom_call" | custom-call | tf_op jit(solution)/shard_map/pallas_call | solution.py:525
  54.0 0.5 slice.194
  55.2 0.0 copy-done.1
  55.2 0.2 conditional.1
  55.4 1.6 %copy.1883 = f32[128,256]{1,0:T(8,128)} copy(f32[128,256]{1,0:T(8,128)} %get-tuple-element.183) | data formatting | bytes 262144
  57.0 1.6 %copy.1884 = f32[128,256]{1,0:T(8,128)} copy(f32[128,256]{1,0:T(8,128)} %get-tuple-element.184) | data formatting | bytes 262144
Async XLA Ops:
  0.6 54.5 %copy-start.1 = (f32[128,256]{1,0:T(8,128)S(1)}, f32[128,256]{1,0:T(8,128)}, u32[]{:S(2)}) copy-start(f32[128,256]{1,0:T(8,128)} %start.1) | copy-start | bytes 393220

commit v3 on v2

--- a/solution.py
+++ b/solution.py
@@ -104,11 +104,26 @@
     def trip(k, carry):
         body([low + step * k + i for i in range(step)])
         return carry
-    lax.fori_loop(0, (high - low) // step, trip, 0)
-
-
-def kernel(nr, nc, elev, start, x_out, r_out, flag, ev, tr, sx, side, side_t, sent, got, sent_s, got_s, cols, fold, wts,
-           s_v, v0, v1, v2, v3, perm, permh, permt, one, two, hs, hr, ls, s1s, s1r, s2s, s2r):
+    full = (high - low) // step
+    lax.fori_loop(0, full, trip, 0)
+    if full * step < high - low:
+        body([jnp.int32(t) for t in range(low + full * step, high)])
+
+
+def edges(top, bottom, step, body):
+    count = top[1] - top[0]
+
+    def tile(k):
+        return jnp.where(k < count, top[0] + k, bottom[0] - count + k)
+
+    def trip(k, carry):
+        body([tile(step * k + i) for i in range(step)])
+        return carry
+    lax.fori_loop(0, (count + bottom[1] - bottom[0]) // step, trip, 0)
+
+
+def kernel(nr, nc, elev, start, xa_out, xb_out, ra_out, rb_out, flag, ev, tr, sx, side, sent_c, got_c, sent, got, sent_s, got_s, cols, fold, wts,
+           s_v, v0, v1, v2, v3, perm, permt, one, two, hs, hr, ls, s1s, s1r, s2s, s2r):
     my_r, my_c = lax.axis_index("row"), lax.axis_index("col")
     rows, width = start.shape
     span = 4 * rows
@@ -141,11 +156,6 @@
     m_i = lax.broadcasted_iota(jnp.int32, (512, 128), 1)
     for q in range(4):
         perm[:, 128 * q:128 * (q + 1)] = jnp.where(n_i == 4 * m_i + q, 1.0, 0.0).astype(BF16)
-    n_h = lax.broadcasted_iota(jnp.int32, (256, 128), 0)
-    m_h = lax.broadcasted_iota(jnp.int32, (256, 128), 1)
-    for q in range(4):
-        hit = ((m_h < 32) & (n_h == 4 * m_h + q)) | ((m_h >= 96) & (n_h == 4 * m_h - 256 + q))
-        permh[:, 128 * q:128 * (q + 1)] = jnp.where(hit, 1.0, 0.0).astype(BF16)
     n_t = lax.broadcasted_iota(jnp.int32, (128, 128), 0)
     m_t = lax.broadcasted_iota(jnp.int32, (128, 128), 1)
     for q in range(4):
@@ -168,8 +178,9 @@
         m = matrix[...]
         y = jnp.dot(hi, m, preferred_element_type=F32) + jnp.dot(mid, m, preferred_element_type=F32)
         y = y + jnp.dot(low, m, preferred_element_type=F32)
-        for q in range(4):
-            tr[3 * q + j, pl.ds(r0, rn), :] = y[:, 128 * q:128 * (q + 1)]
+        for k, first_row in enumerate(r0 if isinstance(r0, tuple) else (r0,)):
+            for q in range(4):
+                tr[4 * j + q, pl.ds(first_row, rn), :] = y[rn * k:rn * (k + 1), 128 * q:128 * (q + 1)]
 
     def gather_own(b, carry):
         r0 = pl.multiple_of(4 * PAD + 128 * b, 64)
@@ -185,19 +196,24 @@
         sent[48:96, 128 * b:128 * (b + 1)] = block[:, 4 * width - 128:4 * width].T[80:128]
     sent_s[0:16, :] = sx[PAD:PAD + rows, 0:128].T[0:16]
     sent_s[16:32, :] = sx[PAD:PAD + rows, width - 128:width].T[112:128]
+    lane_c = lax.broadcasted_iota(jnp.int32, (24, LANES), 1)
+    corners = [(1, 1), (1, -1), (-1, 1), (-1, -1)]
+    for k, (dr, dc) in enumerate(corners):
+        r0 = 4 * PAD + (span - 48 if dr > 0 else 0)
+        q0 = PAD + (rows - 24 if dr > 0 else 0)
+        c0, d0 = (4 * width - LANES, width - LANES) if dc > 0 else (0, 0)
+        high = ev[r0:r0 + 24, c0:c0 + LANES]
+        low = ev[r0 + 24:r0 + 48, c0:c0 + LANES]
+        ctl = sx[q0:q0 + 24, d0:d0 + LANES]
+        if dc > 0:
+            high, low, ctl = pltpu.roll(high, 48, 1), pltpu.roll(low, 96, 1), pltpu.roll(ctl, 112, 1)
+        else:
+            low, ctl = pltpu.roll(low, 48, 1), pltpu.roll(ctl, 96, 1)
+        sent_c[k] = jnp.where(lane_c < 48, high, jnp.where(lane_c < 96, low, ctl))
     lax.fori_loop(0, span // 128, gather_own, 0)
 
     pl.semaphore_wait(barrier, (nr - 1) + (nc - 1) + 4)
 
-    up, down = 48, 40
-    el_from_r = {1: (span - up, up), -1: (0, down)}
-    el_to_r = {1: 4 * PAD - up, -1: 4 * PAD + span}
-    el_from_c = {1: (4 * width - LANES, LANES), -1: (0, LANES), 0: (0, 4 * width)}
-    el_to_c = {1: 4 * width + LANES, -1: 4 * width, 0: 0}
-    s_from_r = {1: (rows - PAD, PAD), -1: (0, PAD)}
-    s_to_r = {1: 0, -1: PAD + rows}
-    s_from_c = {1: (width - LANES, LANES), -1: (0, LANES), 0: (0, width)}
-    s_to_c = {1: width + LANES, -1: width, 0: 0}
     sends = []
 
     def send_to(dr, dc, src, dst):
@@ -207,23 +223,22 @@
             device_id=(wrap(my_r + dr, nr), wrap(my_c + dc, nc)), device_id_type=MESH))
         sends[-1].start()
 
-    for dr, dc in sorted(near, key=lambda o: (o[0] == 0, o[1] != 0)):
-        if dr:
-            for src, dst, fr, tor, fc, toc in ((elev, ev, el_from_r, el_to_r, el_from_c, el_to_c),
-                                               (start, sx, s_from_r, s_to_r, s_from_c, s_to_c)):
-                (r0, rn), (c0, cn) = fr[dr], fc[dc]
-                send_to(dr, dc, src.at[pl.ds(r0, rn), pl.ds(c0, cn)], dst.at[pl.ds(tor[dr], rn), pl.ds(toc[dc], cn)])
-        else:
-            part, to_s = (pl.ds(0, 48), pl.ds(0, 16)) if dc < 0 else (pl.ds(48, 48), pl.ds(112, 16))
-            send_to(dr, dc, sent.at[part], got.at[part])
-            send_to(dr, dc, sent_s.at[pl.ds(0, 16) if dc < 0 else pl.ds(16, 16)], got_s.at[to_s])
-
-    for copy in sends:
+    for dc in (-1, 1):
+        part, part_s, to_s = ((pl.ds(0, 48), pl.ds(0, 16), pl.ds(0, 16)) if dc < 0
+                              else (pl.ds(48, 48), pl.ds(16, 16), pl.ds(112, 16)))
+        send_to(0, dc, sent.at[part], got.at[part])
+        send_to(0, dc, sent_s.at[part_s], got_s.at[to_s])
+    beside_count = len(sends)
+    for k, (dr, dc) in enumerate(corners):
+        send_to(dr, dc, sent_c.at[k], got_c.at[k])
+    up, down = 48, 40
+    send_to(1, 0, start.at[pl.ds(rows - PAD, PAD)], sx.at[pl.ds(0, PAD)])
+    send_to(-1, 0, start.at[pl.ds(0, PAD)], sx.at[pl.ds(PAD + rows, PAD)])
+    send_to(1, 0, tr.at[pl.ds(0, 8), pl.ds(4 * PAD + span - up, up)], tr.at[pl.ds(0, 8), pl.ds(4 * PAD - up, up)])
+    send_to(-1, 0, tr.at[pl.ds(0, 8), pl.ds(4 * PAD, down)], tr.at[pl.ds(0, 8), pl.ds(4 * PAD + span, down)])
+
+    for copy in sends[:beside_count]:
         copy.wait_recv()
-    for r0 in (0, 4 * PAD + span):
-        for j in range(2):
-            gather(ev[r0:r0 + 64, 512 * j:512 * (j + 1)], perm, j, r0, 64)
-        gather(ev[r0:r0 + 64, 4 * width:4 * width + 256], permh, 2, r0, 64)
     for b in range(span // 128):
         gather(got[:, 128 * b:128 * (b + 1)].T, permt, 2, 4 * PAD + 128 * b, 128)
 
@@ -236,10 +251,6 @@
     cell_side = ((lane < 9) & (has_right > 0)) | ((lane >= 116) & (has_left > 0))
 
     side[PAD:PAD + rows, :] = got_s[...].T
-    lane2 = lax.broadcasted_iota(jnp.int32, (PAD, LANES), 1)
-    for r0 in (0, PAD + rows):
-        side[r0:r0 + PAD, :] = jnp.where(
-            lane2 < 64, sx[r0:r0 + PAD, width:width + LANES], sx[r0:r0 + PAD, width + LANES:width + 2 * LANES])
 
     def inside_rows(t):
         g = rows * my_r + 8 * t - PAD + sub
@@ -288,7 +299,7 @@
                     z = expand4([cols[q, j, at(t, a), :] for a in range(4)])
                     y = []
                     for p in range(4):
-                        el = tr[3 * q + j, pl.ds(pl.multiple_of(32 * t, 32) + p, 8, stride=4), :]
+                        el = tr[4 * j + q, pl.ds(pl.multiple_of(32 * t, 32) + p, 8, stride=4), :]
                         misfit = el - 0.25 * z[p]
                         w = huber_delta / jnp.maximum(jnp.abs(misfit), huber_delta)
                         wts[4 * p + q, j, at(t), :] = jnp.where(ok, w * 0.0625, 0.0)
@@ -335,13 +346,13 @@
                     keep_spread(u, t)
         return body
 
-    loop(0, 20, 2, first)
-    loop(0, 20, 1, rows_first)
-    loop(0, 20, UF, finish(s_v, v0, -ridge, True))
-    loop(0, 19, 1, rows_next)
-    loop(1, 19, UF1, finish(v0, v1, ridge - SHIFT, True))
-    loop(1, 19, 1, rows_next)
-    loop(1, 19, UF1, finish(v1, v2, ridge - SHIFT, True))
+    loop(2, 18, 2, first)
+    loop(2, 17, 1, rows_first)
+    loop(3, 17, 4, finish(s_v, v0, -ridge, True))
+    loop(3, 16, 1, rows_next)
+    loop(4, 16, 4, finish(v0, v1, ridge - SHIFT, True))
+    loop(4, 15, 1, rows_next)
+    loop(5, 15, 5, finish(v1, v2, ridge - SHIFT, True))
 
     def moments(t, accs):
         for j in range(2):
@@ -355,7 +366,29 @@
             accs = tuple(x + y for x, y in zip(accs, (a * a, a * b, b * b, b * c, c * c, energy)))
         return accs
 
-    accs = lax.fori_loop(own_low, own_high, moments, (zero,) * 6)
+    accs = lax.fori_loop(5, 14, moments, (zero,) * 6)
+
+    for copy in sends[beside_count:]:
+        copy.wait_recv()
+    lane2 = lax.broadcasted_iota(jnp.int32, (PAD, LANES), 1)
+    lane_d = lax.broadcasted_iota(jnp.int32, (48, LANES), 1)
+    turned = []
+    for k, (q0, cut) in enumerate(((0, 8), (PAD + rows, 0))):
+        from_left, from_right = got_c[2 * k], got_c[2 * k + 1]
+        left2 = jnp.concatenate([pltpu.roll(from_left, 48, 1), from_left], 0)
+        right2 = jnp.concatenate([from_right, pltpu.roll(from_right, 80, 1)], 0)
+        turned.append(jnp.where(lane_d < 48, right2, left2))
+        side[q0:q0 + PAD, :] = jnp.where(
+            lane2 < 64, pltpu.roll(from_right[cut:cut + PAD], 32, 1), pltpu.roll(from_left[cut:cut + PAD], 16, 1))
+    gather(jnp.concatenate(turned, 0), permt, 2, (4 * PAD - 48, 4 * PAD + span), 48)
+    edges((0, 2), (18, 20), 4, first)
+    edges((0, 2), (17, 20), 1, rows_first)
+    edges((0, 3), (17, 20), 6, finish(s_v, v0, -ridge, True))
+    edges((0, 3), (16, 19), 1, rows_next)
+    edges((1, 4), (16, 19), 6, finish(v0, v1, ridge - SHIFT, True))
+    edges((1, 4), (15, 19), 1, rows_next)
+    edges((1, 5), (15, 19), 8, finish(v1, v2, ridge - SHIFT, True))
+    accs = lax.fori_loop(0, 7, lambda k, a: moments(jnp.where(k < 3, 2 + k, 11 + k), a), accs)
 
     for k, acc in enumerate(accs):
         one[my_c, k:k + 1, :] = jnp.sum(acc, axis=0, keepdims=True)
@@ -385,7 +418,7 @@
     loop(1, 18, 1, rows_next)
     two[my_r] = arrive(one, s1s, s1r, my_c, nc, lambda s: (my_r, s))
     sends += exchange(two, s2s, s2r, my_r, nr, lambda s: (s, my_c))
-    loop(2, 18, UF2, finish(v2, v3, ridge - SHIFT, False))
+    loop(2, 18, 4, finish(v2, v3, ridge - SHIFT, False))
     total = arrive(two, s2s, s2r, my_r, nr, lambda s: (s, my_c))
     total = jnp.broadcast_to(jnp.sum(total, axis=1, keepdims=True), (8, LANES))
     nu = [total[k:k + 1, :] for k in range(6)]
@@ -394,24 +427,24 @@
     step, last, fine = cg_scalars(pairs)
 
     step, last = ([jnp.broadcast_to(k, (8, LANES)) for k in ks] for ks in (step, last))
-    flag[...] = jnp.broadcast_to(fine, (8, LANES))
+    flag[0, 0] = jnp.max(fine)
+    use = jnp.broadcast_to(fine, (8, LANES)) > 0.5
 
     def final(ts):
         for t in ts:
             out_rows = pl.ds(pl.multiple_of(8 * t, 8) - PAD, 8)
             for j in range(2):
                 v = [ref[j, at(t), :] for ref in (v0, v1, v2, v3)]
-                x_out[out_rows, 128 * j:128 * (j + 1)] = (
-                    s_v[j, at(t), :] + ((step[0] * v[0] + step[1] * v[1]) + step[2] * v[2]))
-                r_out[out_rows, 128 * j:128 * (j + 1)] = (
-                    (last[0] * v[0] + last[1] * v[1]) + (last[2] * v[2] + last[3] * v[3]))
+                xa = (step[0] * v[0] + step[1] * v[1]) + step[2] * v[2]
+                xa_out[out_rows, 128 * j:128 * (j + 1)] = jnp.where(use, xa, 0.0)
+                xb_out[out_rows, 128 * j:128 * (j + 1)] = s_v[j, at(t), :]
+                ra_out[out_rows, 128 * j:128 * (j + 1)] = jnp.where(use, last[0] * v[0] + last[1] * v[1], 0.0)
+                rb_out[out_rows, 128 * j:128 * (j + 1)] = last[2] * v[2] + last[3] * v[3]
 
     loop(own_low, own_high, 2, final)
     for copy in sends:
         copy.wait_send()
 
-
-UF, UF1, UF2 = 4, 3, 4
 
 def from_behind(block, axis, distance):
     devices = range(lax.axis_size(axis))
@@ -522,17 +555,18 @@
         out = jax.ShapeDtypeStruct((rows, width), F32)
         tall = rows + 2 * PAD
         field = pltpu.VMEM((3, tall, LANES), F32)
-        x, r, fine = pl.pallas_call(
+        xa, xb, ra, rb, fine = pl.pallas_call(
             functools.partial(kernel, nr, nc),
-            out_shape=(out, out, jax.ShapeDtypeStruct((8, LANES), F32)),
+            out_shape=(out, out, out, out, jax.ShapeDtypeStruct((1, 1), F32)),
             in_specs=[pl.BlockSpec(memory_space=pltpu.HBM)] * 2,
-            out_specs=(pl.BlockSpec(memory_space=pltpu.VMEM),) * 3,
+            out_specs=(pl.BlockSpec(memory_space=pltpu.VMEM),) * 4 + (pl.BlockSpec(memory_space=pltpu.SMEM),),
             scratch_shapes=[
-                pltpu.VMEM((4 * tall, 4 * width + 2 * LANES), F32),
+                pltpu.VMEM((4 * tall, 4 * width), F32),
                 pltpu.VMEM((12, 4 * tall, LANES), F32),
-                pltpu.VMEM((tall, width + 2 * LANES), F32),
+                pltpu.VMEM((tall, width), F32),
                 pltpu.VMEM((tall, LANES), F32),
-                pltpu.VMEM((8, LANES), F32),
+                pltpu.VMEM((4, 24, LANES), F32),
+                pltpu.VMEM((4, 24, LANES), F32),
                 pltpu.VMEM((96, 4 * rows), F32),
                 pltpu.VMEM((128, 4 * rows), F32),
                 pltpu.VMEM((32, rows), F32),
@@ -542,7 +576,6 @@
                 pltpu.VMEM((16, 3, tall, LANES), F32),
                 field, field, field, field, field,
                 pltpu.VMEM((512, 512), BF16),
-                pltpu.VMEM((256, 512), BF16),
                 pltpu.VMEM((128, 512), BF16),
                 pltpu.VMEM((nc, 8, LANES), F32),
                 pltpu.VMEM((nr, 8, LANES), F32),
@@ -555,10 +588,11 @@
                 pltpu.SemaphoreType.DMA((nr,)),
             ],
             compiler_params=pltpu.CompilerParams(
-                collective_id=0, has_side_effects=True, vmem_limit_bytes=50 * 1024 * 1024
+                collective_id=0, has_side_effects=True, vmem_limit_bytes=60 * 1024 * 1024
             ),
         )(elevation, start_controls)
-        return lax.cond(fine[0, 0] > 0.5, lambda: (x, r), lambda: step_by_step(elevation, start_controls))
+        x, r = lax.cond(fine[0, 0] > 0.5, lambda: (xb, rb), lambda: step_by_step(elevation, start_controls))
+        return xa + x, ra + r
 
     return jax.shard_map(
         shards,

time: 58.7 us -> 49.3 us (0.84)
  Pallas kernels: 53.4 us -> 44.4 us
  local copies, waits for them, and re-layouts: 3.65 us -> 0.01 us
  other arithmetic: 0 us -> 3.28 us
    pallas_call x1, Pallas kernels: 53.4 us -> 44.4 us  [shards(): pl.pallas_call(functools.partial(kernel, nr, nc), out_shape=(out, out, ou...]
    add x0 -> x2, other arithmetic: none -> 3.28 us  [shards(): return (xa + x, ra + r)]
    unnamed x4 -> x2, local copies, waits for them, and re-layouts: 3.14 us -> 0.01 us
where the time goes in v3:
time: 49.3 us; the launch traced here: 49.2 us
  Pallas kernels  44.4 us (90%)
  other arithmetic  3.28 us (7%)
  between operations  1.22 us (2%)
    pallas_call x1, Pallas kernels, shards(): pl.pallas_call(functools.partial(kernel, nr, nc), out_shape=(out, out, ou...  44.4 us
    add x2, other arithmetic, shards(): return (xa + x, ra + r)  3.28 us

profile of v3, /device:TPU:1, one launch (start us, length us, event | category | flops | bytes accessed | tf_op | source)
XLA Modules:
  0.0 49.2 jit_solution(9982943291281388066)
XLA Ops:
  0.6 0.0 copy-start.2
  0.6 44.4 %shard_map.41 = (f32[128,256]{1,0:T(8,128)}, f32[128,256]{1,0:T(8,128)}, f32[128,256]{1,0:T(8,128)}, f32[128,256]{1,0:T(8,128)}, f32[1,1]{1,0:T(1,128)}) custom-call(f32[512,1024]{1,0:T(8,128)} %elev.1, f32[128,256]{1,0:T(8,128)} %start.1), custom_call_target="tpu_custom_call" | custom-call | tf_op jit(solution)/shard_map/pallas_call | solution.py:558
  45.6 0.0 copy-done.2
  45.6 0.2 conditional.1
  45.9 1.6 %add.938 = f32[128,256]{1,0:T(8,128)} add(f32[128,256]{1,0:T(8,128)} %get-tuple-element.19, f32[128,256]{1,0:T(8,128)} %get-tuple-element.66) | non-fusion elementwise | flops 32768 | bytes 393216 | tf_op jit(solution)/shard_map/add | solution.py:595
  47.5 1.6 %add.939 = f32[128,256]{1,0:T(8,128)} add(f32[128,256]{1,0:T(8,128)} %get-tuple-element.24, f32[128,256]{1,0:T(8,128)} %get-tuple-element.67) | non-fusion elementwise | flops 32768 | bytes 393216 | tf_op jit(solution)/shard_map/add | solution.py:595
Async XLA Ops:
  0.6 45.0 %copy-start.2 = (f32[128,256]{1,0:T(8,128)S(1)}, f32[128,256]{1,0:T(8,128)}, u32[]{:S(2)}) copy-start(f32[128,256]{1,0:T(8,128)} %start.1) | copy-start | bytes 393220

commit v4 on v3

--- a/solution.py
+++ b/solution.py
@@ -346,7 +346,7 @@
                     keep_spread(u, t)
         return body
 
-    loop(2, 18, 2, first)
+    loop(2, 18, 4, first)
     loop(2, 17, 1, rows_first)
     loop(3, 17, 4, finish(s_v, v0, -ridge, True))
     loop(3, 16, 1, rows_next)
@@ -419,6 +419,8 @@
     two[my_r] = arrive(one, s1s, s1r, my_c, nc, lambda s: (my_r, s))
     sends += exchange(two, s2s, s2r, my_r, nr, lambda s: (s, my_c))
     loop(2, 18, 4, finish(v2, v3, ridge - SHIFT, False))
+    for copy in sends[:-(nr - 1)]:
+        copy.wait_send()
     total = arrive(two, s2s, s2r, my_r, nr, lambda s: (s, my_c))
     total = jnp.broadcast_to(jnp.sum(total, axis=1, keepdims=True), (8, LANES))
     nu = [total[k:k + 1, :] for k in range(6)]
@@ -441,8 +443,8 @@
                 ra_out[out_rows, 128 * j:128 * (j + 1)] = jnp.where(use, last[0] * v[0] + last[1] * v[1], 0.0)
                 rb_out[out_rows, 128 * j:128 * (j + 1)] = last[2] * v[2] + last[3] * v[3]
 
-    loop(own_low, own_high, 2, final)
-    for copy in sends:
+    loop(own_low, own_high, 4, final)
+    for copy in sends[-(nr - 1):]:
         copy.wait_send()
 
 
@@ -545,6 +547,11 @@
         direction = residual + norm_next / norm_now * direction
         norm_now = norm_next
     return (controls, residual)
+
+
+def add_pairs(xa, xb, ra, rb, x, r):
+    x[...] = xa[...] + xb[...]
+    r[...] = ra[...] + rb[...]
 
 
 def solution(mesh):
@@ -592,7 +599,7 @@
             ),
         )(elevation, start_controls)
         x, r = lax.cond(fine[0, 0] > 0.5, lambda: (xb, rb), lambda: step_by_step(elevation, start_controls))
-        return xa + x, ra + r
+        return pl.pallas_call(add_pairs, out_shape=(out, out))(xa, x, ra, r)
 
     return jax.shard_map(
         shards,

time: 49.3 us -> 47.4 us (0.961)
  other arithmetic: 3.28 us -> 0 us
  Pallas kernels: 44.4 us -> 45.8 us
    add x2 -> x0, other arithmetic: 3.28 us -> none  [shards(): return (xa + x, ra + r)]
    pallas_call x0 -> x1, Pallas kernels: none -> 1.81 us  [shards(): return pl.pallas_call(add_pairs, out_shape=(out, out))(xa, x, ra, r)]
where the time goes in v4:
time: 47.4 us; the launch traced here: 47.3 us
  Pallas kernels  45.8 us (97%)
  between operations  1.22 us (3%)
    pallas_call x1, Pallas kernels, shards(): pl.pallas_call(functools.partial(kernel, nr, nc), out_shape=(out, out, ou...  44 us
    pallas_call x1, Pallas kernels, shards(): return pl.pallas_call(add_pairs, out_shape=(out, out))(xa, x, ra, r)  1.81 us

profile of v4, /device:TPU:1, one launch (start us, length us, event | category | flops | bytes accessed | tf_op | source)
XLA Modules:
  0.0 47.3 jit_solution(9183735332461069581)
XLA Ops:
  0.6 0.0 copy-start.2
  0.6 44.0 %shard_map.41 = (f32[128,256]{1,0:T(8,128)}, f32[128,256]{1,0:T(8,128)}, f32[128,256]{1,0:T(8,128)}, f32[128,256]{1,0:T(8,128)}, f32[1,1]{1,0:T(1,128)}) custom-call(f32[512,1024]{1,0:T(8,128)} %elev.1, f32[128,256]{1,0:T(8,128)} %start.1), custom_call_target="tpu_custom_call" | custom-call | tf_op jit(solution)/shard_map/pallas_call | solution.py:565
  45.2 0.0 copy-done.2
  45.2 0.2 conditional.1
  45.5 1.8 %shard_map.42 = (f32[128,256]{1,0:T(8,128)}, f32[128,256]{1,0:T(8,128)}) custom-call(f32[128,256]{1,0:T(8,128)} %get-tuple-element.19.xa, f32[128,256]{1,0:T(8,128)} %get-tuple-element.66.xb, f32[128,256]{1,0:T(8,128)} %get-tuple-element.24.ra, f32[128,256]{1,0:T(8,128)} %get-tuple-element.67.rb), custom_call_target="tpu_custom_call" | custom-call | tf_op jit(solution)/shard_map/pallas_call | solution.py:602
Async XLA Ops:
  0.6 44.6 %copy-start.2 = (f32[128,256]{1,0:T(8,128)S(1)}, f32[128,256]{1,0:T(8,128)}, u32[]{:S(2)}) copy-start(f32[128,256]{1,0:T(8,128)} %start.1) | copy-start | bytes 393220

commit v5 on v4

--- a/solution.py
+++ b/solution.py
@@ -210,37 +210,6 @@
         else:
             low, ctl = pltpu.roll(low, 48, 1), pltpu.roll(ctl, 96, 1)
         sent_c[k] = jnp.where(lane_c < 48, high, jnp.where(lane_c < 96, low, ctl))
-    lax.fori_loop(0, span // 128, gather_own, 0)
-
-    pl.semaphore_wait(barrier, (nr - 1) + (nc - 1) + 4)
-
-    sends = []
-
-    def send_to(dr, dc, src, dst):
-        k = len(sends)
-        sends.append(pltpu.make_async_remote_copy(
-            src_ref=src, dst_ref=dst, send_sem=hs.at[k], recv_sem=hr.at[k],
-            device_id=(wrap(my_r + dr, nr), wrap(my_c + dc, nc)), device_id_type=MESH))
-        sends[-1].start()
-
-    for dc in (-1, 1):
-        part, part_s, to_s = ((pl.ds(0, 48), pl.ds(0, 16), pl.ds(0, 16)) if dc < 0
-                              else (pl.ds(48, 48), pl.ds(16, 16), pl.ds(112, 16)))
-        send_to(0, dc, sent.at[part], got.at[part])
-        send_to(0, dc, sent_s.at[part_s], got_s.at[to_s])
-    beside_count = len(sends)
-    for k, (dr, dc) in enumerate(corners):
-        send_to(dr, dc, sent_c.at[k], got_c.at[k])
-    up, down = 48, 40
-    send_to(1, 0, start.at[pl.ds(rows - PAD, PAD)], sx.at[pl.ds(0, PAD)])
-    send_to(-1, 0, start.at[pl.ds(0, PAD)], sx.at[pl.ds(PAD + rows, PAD)])
-    send_to(1, 0, tr.at[pl.ds(0, 8), pl.ds(4 * PAD + span - up, up)], tr.at[pl.ds(0, 8), pl.ds(4 * PAD - up, up)])
-    send_to(-1, 0, tr.at[pl.ds(0, 8), pl.ds(4 * PAD, down)], tr.at[pl.ds(0, 8), pl.ds(4 * PAD + span, down)])
-
-    for copy in sends[:beside_count]:
-        copy.wait_recv()
-    for b in range(span // 128):
-        gather(got[:, 128 * b:128 * (b + 1)].T, permt, 2, 4 * PAD + 128 * b, 128)
 
     lane = lax.broadcasted_iota(jnp.int32, (8, LANES), 1)
     sub = lax.broadcasted_iota(jnp.int32, (8, LANES), 0)
@@ -250,8 +219,6 @@
     beside_f = jnp.where(beside, 1.0, 0.0)
     cell_side = ((lane < 9) & (has_right > 0)) | ((lane >= 116) & (has_left > 0))
 
-    side[PAD:PAD + rows, :] = got_s[...].T
-
     def inside_rows(t):
         g = rows * my_r + 8 * t - PAD + sub
         return (g >= 0) & (g < nr * rows)
@@ -271,12 +238,20 @@
         x = [v] + [left_shift(v, c) for c in range(1, 4)]
         return [expand4([x[c][j] for c in range(4)]) for j in range(3)]
 
-    def keep_spread(u, t):
-        for j in range(3):
+    def keep_spread(u, t, js=(0, 1, 2)):
+        for j in js:
             for q in range(4):
                 cols[q, j, at(t), :] = u[j][q]
 
-    def first(ts):
+    def first_near(ts):
+        done = []
+        for t in ts:
+            v = [jnp.where(inside_rows(t), sx[at(t), 128 * j:128 * (j + 1)], 0.0) for j in range(2)]
+            done.append((t, spread(v + [v[1]])))
+        for t, u in done:
+            keep_spread(u, t, (0,))
+
+    def first(ts, js=(0, 1, 2)):
         done = []
         for t in ts:
             keep = inside_rows(t)
@@ -287,13 +262,13 @@
         for t, v, u in done:
             for j in range(3):
                 s_v[j, at(t), :] = v[j]
-            keep_spread(u, t)
-
-    def rows_first(ts):
+            keep_spread(u, t, js)
+
+    def rows_first(ts, js=(0, 1, 2)):
         for t in ts:
             i = 8 * t + sub
             okr = inside_rows(t) & (i >= PAD - 12) & (i < PAD + rows + 9)
-            for j in range(3):
+            for j in js:
                 ok = okr & cell_side if j == 2 else okr
                 for q in range(4):
                     z = expand4([cols[q, j, at(t, a), :] for a in range(4)])
@@ -346,12 +321,48 @@
                     keep_spread(u, t)
         return body
 
-    loop(2, 18, 4, first)
-    loop(2, 17, 1, rows_first)
+    pl.semaphore_wait(barrier, (nr - 1) + (nc - 1) + 4)
+
+    sends = []
+
+    def send_to(dr, dc, src, dst):
+        k = len(sends)
+        sends.append(pltpu.make_async_remote_copy(
+            src_ref=src, dst_ref=dst, send_sem=hs.at[k], recv_sem=hr.at[k],
+            device_id=(wrap(my_r + dr, nr), wrap(my_c + dc, nc)), device_id_type=MESH))
+        sends[-1].start()
+
+    for dc in (-1, 1):
+        part, part_s, to_s = ((pl.ds(0, 48), pl.ds(0, 16), pl.ds(0, 16)) if dc < 0
+                              else (pl.ds(48, 48), pl.ds(16, 16), pl.ds(112, 16)))
+        send_to(0, dc, sent.at[part], got.at[part])
+        send_to(0, dc, sent_s.at[part_s], got_s.at[to_s])
+    beside_count = len(sends)
+    for k, (dr, dc) in enumerate(corners):
+        send_to(dr, dc, sent_c.at[k], got_c.at[k])
+    up, down = 48, 40
+    send_to(1, 0, start.at[pl.ds(rows - PAD, PAD)], sx.at[pl.ds(0, PAD)])
+    send_to(-1, 0, start.at[pl.ds(0, PAD)], sx.at[pl.ds(PAD + rows, PAD)])
+    blocks = span // 128
+    lax.fori_loop(0, 2, lambda k, c: gather_own(k * (blocks - 1), c), 0)
+    send_to(1, 0, tr.at[pl.ds(0, 8), pl.ds(4 * PAD + span - up, up)], tr.at[pl.ds(0, 8), pl.ds(4 * PAD - up, up)])
+    send_to(-1, 0, tr.at[pl.ds(0, 8), pl.ds(4 * PAD, down)], tr.at[pl.ds(0, 8), pl.ds(4 * PAD + span, down)])
+
+    lax.fori_loop(1, blocks - 1, gather_own, 0)
+    loop(2, 18, 4, first_near)
+    loop(2, 17, 3, lambda ts: rows_first(ts, (0,)))
+    for copy in sends[:beside_count]:
+        copy.wait_recv()
+    for b in range(span // 128):
+        gather(got[:, 128 * b:128 * (b + 1)].T, permt, 2, 4 * PAD + 128 * b, 128)
+    side[PAD:PAD + rows, :] = got_s[...].T
+
+    loop(2, 18, 4, lambda ts: first(ts, (1, 2)))
+    loop(2, 17, 3, lambda ts: rows_first(ts, (1, 2)))
     loop(3, 17, 4, finish(s_v, v0, -ridge, True))
-    loop(3, 16, 1, rows_next)
+    loop(3, 16, 2, rows_next)
     loop(4, 16, 4, finish(v0, v1, ridge - SHIFT, True))
-    loop(4, 15, 1, rows_next)
+    loop(4, 15, 2, rows_next)
     loop(5, 15, 5, finish(v1, v2, ridge - SHIFT, True))
 
     def moments(t, accs):
@@ -384,7 +395,7 @@
     edges((0, 2), (18, 20), 4, first)
     edges((0, 2), (17, 20), 1, rows_first)
     edges((0, 3), (17, 20), 6, finish(s_v, v0, -ridge, True))
-    edges((0, 3), (16, 19), 1, rows_next)
+    edges((0, 3), (16, 19), 2, rows_next)
     edges((1, 4), (16, 19), 6, finish(v0, v1, ridge - SHIFT, True))
     edges((1, 4), (15, 19), 1, rows_next)
     edges((1, 5), (15, 19), 8, finish(v1, v2, ridge - SHIFT, True))

time: 47.4 us -> 44.6 us (0.941)
  Pallas kernels: 45.8 us -> 43 us
    pallas_call x1, Pallas kernels: 44 us -> 41.2 us  [shards(): pl.pallas_call(functools.partial(kernel, nr, nc), out_shape=(out, out, ou...]
where the time goes in v5:
time: 44.6 us; the launch traced here: 44.5 us
  Pallas kernels  43 us (96%)
  between operations  1.22 us (3%)
    pallas_call x1, Pallas kernels, shards(): pl.pallas_call(functools.partial(kernel, nr, nc), out_shape=(out, out, ou...  41.2 us
    pallas_call x1, Pallas kernels, shards(): return pl.pallas_call(add_pairs, out_shape=(out, out))(xa, x, ra, r)  1.81 us

profile of v5, /device:TPU:1, one launch (start us, length us, event | category | flops | bytes accessed | tf_op | source)
XLA Modules:
  0.0 44.5 jit_solution(14981976700822196959)
XLA Ops:
  0.6 0.0 copy-start.2
  0.6 41.2 %shard_map.41 = (f32[128,256]{1,0:T(8,128)}, f32[128,256]{1,0:T(8,128)}, f32[128,256]{1,0:T(8,128)}, f32[128,256]{1,0:T(8,128)}, f32[1,1]{1,0:T(1,128)}) custom-call(f32[512,1024]{1,0:T(8,128)} %elev.1, f32[128,256]{1,0:T(8,128)} %start.1), custom_call_target="tpu_custom_call" | custom-call | tf_op jit(solution)/shard_map/pallas_call | solution.py:576
  42.4 0.0 copy-done.2
  42.4 0.2 conditional.1
  42.7 1.8 %shard_map.42 = (f32[128,256]{1,0:T(8,128)}, f32[128,256]{1,0:T(8,128)}) custom-call(f32[128,256]{1,0:T(8,128)} %get-tuple-element.19.xa, f32[128,256]{1,0:T(8,128)} %get-tuple-element.66.xb, f32[128,256]{1,0:T(8,128)} %get-tuple-element.24.ra, f32[128,256]{1,0:T(8,128)} %get-tuple-element.67.rb), custom_call_target="tpu_custom_call" | custom-call | tf_op jit(solution)/shard_map/pallas_call | solution.py:613
Async XLA Ops:
  0.6 41.8 %copy-start.2 = (f32[128,256]{1,0:T(8,128)S(1)}, f32[128,256]{1,0:T(8,128)}, u32[]{:S(2)}) copy-start(f32[128,256]{1,0:T(8,128)} %start.1) | copy-start | bytes 393220
